TPU v7x, 256 devices: a whole 4x4x8 slice. The times are simulated.
256 devices in a mesh: dp: 16 (over y_hi, x, core), mp: 16 (over y_lo, z).
Axes of the slice: x: 4, y: 4 (y_hi: 2, y_lo: 2; y = y_hi * 2 + y_lo), z: 8, core: 2. Of those that a mesh axis runs over, the one named last changes fastest.
Arguments:
- activations: bfloat16 [4096, 4096], P('dp', 'mp'), may hold values from -6 to 6
- output_grads: bfloat16 [4096, 32768], P('dp', 'mp'), may hold values from -0.09375 to 0.09375
- owners: int32 [16, 16], replicated, may hold values from 0 to 15, as said below
- statistics: float32 [16, 16, 1024, 1024], P('mp', 'dp'), may hold values from -3 to 8
- inv_roots: bfloat16 [16, 16, 1024, 1024], P('mp', 'dp'), may hold values from -3 to 6
Outputs:
- new_statistics: float32 [16, 16, 1024, 1024], P('mp', 'dp')
- preconditioned: bfloat16 [4096, 32768], P('dp', 'mp')
Inputs may be any that keep to these rules, and one draw needn't show every extreme that they name: `owners`: each row holds every number of 0 to 15 once; entries 2b and 2b + 1 are 2k and 2k + 1 in some order, for some k.
All inputs are finite; a program needn't handle non-finite values.
Results may differ from a plain program's by a relative error of at most 0.024.
Values may be sent and summed in bfloat16 or wider, within the bound.
No kernel may reach another device: no remote copies, remote signals or barrier semaphores. Data moves between devices by JAX's collectives and lax.ppermute only.
A program may use at most 128 MiB of HBM per device.

v0:
```python
import jax
import jax.numpy as jnp
from jax import lax
from jax.experimental import pallas as pl
from jax.experimental.pallas import tpu as pltpu
from jax.sharding import PartitionSpec as P

BLK = 1024
BF = jnp.bfloat16
F32 = jnp.float32
VMEM_LIMIT = 24 * 1024 * 1024

in_vmem = pl.BlockSpec(memory_space=pltpu.VMEM)
in_smem = pl.BlockSpec(memory_space=pltpu.SMEM)
anywhere = pl.BlockSpec(memory_space=pl.ANY)


def call(kernel, outs, ins, in_specs, scratch=(), flops=0, traffic=0, **kw):
    return pl.pallas_call(
        kernel,
        out_shape=outs,
        in_specs=in_specs,
        out_specs=kw.pop("out_specs", jax.tree.map(lambda _: in_vmem, outs)),
        scratch_shapes=list(scratch),
        compiler_params=pltpu.CompilerParams(vmem_limit_bytes=VMEM_LIMIT),
        cost_estimate=pl.CostEstimate(flops=flops, bytes_accessed=traffic, transcendentals=0),
        **kw,
    )(*ins)


def dp_move(v, dy, dx, dc):
    pairs = []
    for y in range(2):
        for x in range(4):
            for c in range(2):
                src = (y * 4 + x) * 2 + c
                dst = ((y ^ dy) * 4 + (x + dx) % 4) * 2 + (c ^ dc)
                pairs.append((src, dst))
    return lax.ppermute(v, "dp", pairs)


def mp_move(v, dy, dz):
    pairs = [(y * 8 + z, (y ^ dy) * 8 + (z + dz) % 8) for y in range(2) for z in range(8)]
    return lax.ppermute(v, "mp", pairs)


def rows(v, start, size):
    return lax.dynamic_slice_in_dim(v, start, size, 0)


def place():
    dp = lax.axis_index("dp")
    mp = lax.axis_index("mp")
    return dp, mp, dp >> 3, (dp >> 1) & 3, dp & 1, mp >> 3, mp & 7


def side_move(v, axis, dy=0):
    pairs = []
    for d in range(16):
        for m in range(16):
            y, x, c, yl, z = d // 8, d // 2 % 4, d % 2, m // 8, m % 8
            step = 1 - 2 * c
            tx = (x + step) % 4 if axis == "x" else x
            tz = (z + step) % 8 if axis == "z" else z
            pairs.append((d * 16 + m, ((y * 4 + tx) * 2 + c) * 16 + (yl ^ dy) * 8 + tz))
    return lax.ppermute(v, ("dp", "mp"), pairs)


def after(value, *tokens, cost=0):
    def kernel(*refs):
        pass

    return call(
        kernel,
        jax.ShapeDtypeStruct(value.shape, value.dtype),
        (value, *tokens),
        [anywhere] * (1 + len(tokens)),
        out_specs=anywhere,
        input_output_aliases={0: 0},
        flops=cost,
    )


def turned(activations):
    def kernel(acts, o0, o1, o2, o3, scratch):
        _, _, _, x, _, _, _ = place()
        scratch[...] = acts[...].T
        for d, out in enumerate((o0, o1, o2, o3)):
            out[...] = scratch[pl.ds(pl.multiple_of(((x + d) & 3) * 64, 64), 64), :]

    return call(
        kernel,
        (jax.ShapeDtypeStruct((64, 256), BF),) * 4,
        (activations,),
        [in_vmem],
        scratch=[pltpu.VMEM((256, 256), BF)],
        traffic=1 << 18,
    )


def side_by_side(parts):
    def kernel(a, b, c, d, out):
        for k, ref in enumerate((a, b, c, d)):
            out[:, k * 256 : k * 256 + 256] = ref[...]

    return call(kernel, jax.ShapeDtypeStruct((64, 1024), BF), parts, [in_vmem] * 4, traffic=1 << 18)


def by_core(half, other):
    def kernel(half, other, out, own):
        c = lax.axis_index("dp") & 1
        out[:, pl.ds(pl.multiple_of(c * 1024, 1024), 1024)] = half[...]
        out[:, pl.ds(pl.multiple_of(1024 - c * 1024, 1024), 1024)] = other[...]
        own[...] = out[pl.ds(pl.multiple_of(c * 32, 32), 32), :]

    return call(
        kernel,
        (jax.ShapeDtypeStruct((64, 2048), BF), jax.ShapeDtypeStruct((32, 2048), BF)),
        (half, other),
        [in_vmem] * 2,
        traffic=1 << 19,
    )


def split(*chunks):
    n = len(chunks)

    def kernel(*refs):
        c = lax.axis_index("dp") & 1
        kept, given = refs[n:]
        for k in range(n):
            kept[k] = refs[k][pl.ds(pl.multiple_of(c * 32, 32), 32), :]
            given[k] = refs[k][pl.ds(pl.multiple_of(32 - c * 32, 32), 32), :]

    out = jax.ShapeDtypeStruct((n, 32, 2048), BF)
    return call(kernel, (out, out), chunks, [in_vmem] * n, traffic=n << 18)


def copied(value, token):
    def kernel(value, token, out):
        out[...] = value[...]

    return call(
        kernel, jax.ShapeDtypeStruct(value.shape, value.dtype), (value, token), [in_vmem, anywhere], traffic=2 << 20
    )


def swapped(a, b, token):
    def kernel(a, b, token, out):
        out[0] = a[...]
        out[1] = b[...]

    both = call(
        kernel, jax.ShapeDtypeStruct((2, 256, 2048), BF), (a, b, token), [in_vmem] * 2 + [anywhere], traffic=4 << 20
    )
    both = dp_move(both, 0, 0, 1)
    return both[0], both[1]


def gather(activations, output_grads):
    own_other = dp_move(output_grads, 0, 0, 1)
    own, plus, two, minus = turned(activations)
    left = dp_move(plus, 0, 1, 0)
    right = dp_move(minus, 0, -1, 0)
    opposite = dp_move(two, 0, 2, 0)
    half = side_by_side((own, left, right, opposite))
    grads = copied(output_grads, half)
    own_other = after(own_other, half)
    near0 = side_move(grads, "x")
    near1 = side_move(own_other, "x")

    chunk, own = by_core(half, dp_move(half, 0, 0, 1))
    own_y = mp_move(own, 1, 0)
    out = [(own[None], (0,), 0, 0), (own_y[None], (0,), 1, 0)]
    tokens = {1: (own_other,), 2: (own_other,), 3: (own_other,)}
    for k in (1, 2, 3):
        chunk = side_move(after(chunk, *tokens[k]), "z")
        kept, given = split(chunk)
        if k == NT:
            token = kept
        given = dp_move(given, 0, 0, 1)
        if k == 3:
            kept = after(kept, near1, first_y) if T1 else after(kept, first_y)
        if k == 2:
            far = side_move(copied(near0, given if FT else kept), "x")
        pair_y = mp_move(jnp.concatenate([kept, given], 0), 1, 0)
        out += [(kept, (k,), 0, 0), (given, (k,), 0, 1), (pair_y, (k, -k), 1, 0)]
        if k == 1:
            first_y = pair_y
    out += [(side_move(kept[0], "z")[None], (4,), 0, 0), (side_move(kept[0], "z", 1)[None], (4,), 1, 0)]
    return out, [output_grads, own_other, near0, near1, *swapped(near0, near1, token), far]


def block_sums(owners, chunks, pieces, *tokens):
    n = len(chunks)

    def kernel(owners, *refs):
        own, own_other, near0, near1, near0_other, near1_other, far, far_other = refs[n : n + 8]
        outs, blocks, feats = refs[-10:-2], refs[-2], refs[-1]
        _, mp, yh, x, c, yl, z = place()
        for ref, (_, distances, dy, crossed) in zip(refs[:n], chunks):
            for k, dist in enumerate(distances):
                dz = dist * (2 * (c ^ crossed) - 1)
                m = (yl ^ (dy[k] if isinstance(dy, tuple) else dy)) * 8 + ((z + dz) & 7)
                feats[pl.ds(pl.multiple_of(m * 32, 32), 32), :] = ref[k]
        parts = [
            (own, 0, 0),
            (own_other, 0, 1),
            (near0, 1 + c, 0),
            (near1, 1 + c, 1),
            (near0_other, 2 - c, 1),
            (near1_other, 2 - c, 0),
            (far, 3, 0),
            (far_other, 3, 1),
        ]
        for j in range(2):
            slots = []
            for r in range(4):
                pair = owners[mp, (r * 2 + j) * 2] >> 1
                slots.append(((pair >> 2) ^ yh) * 4 + ((pair - x) & 3))

            def step(n, _):
                total = jnp.zeros((512, 256), F32)
                for ref, k, other in parts:
                    tokens = (c ^ other) * 1024 + k * 256
                    total += jnp.dot(
                        feats[:, pl.ds(pl.multiple_of(tokens, 256), 256)],
                        ref[:, pl.ds(pl.multiple_of(j * BLK + n * 256, 256), 256)],
                        preferred_element_type=F32,
                    )
                total = total.astype(BF)
                for r in range(4):
                    blocks[slots[r], :, pl.ds(pl.multiple_of(n * 256, 256), 256)] = total[r * 128 : r * 128 + 128]
                return 0

            lax.fori_loop(0, 4, step, 0)
        for k in range(8):
            outs[k][...] = blocks[k]

    return call(
        kernel,
        (jax.ShapeDtypeStruct((128, BLK), BF),) * 8,
        (owners, *[chunk[0] for chunk in chunks], *pieces, *tokens),
        [in_smem] + [in_vmem] * (n + 8) + [anywhere] * len(tokens),
        scratch=[pltpu.VMEM((8, 128, BLK), BF), pltpu.VMEM((512, 2048), BF)],
        flops=4 << 30,
        traffic=8 << 20,
    )


def add(parts):
    def kernel(*refs):
        out = refs[8]
        for k in range(4):
            out[k] = (refs[k][...].astype(F32) + refs[4 + k][...].astype(F32)).astype(BF)

    return call(kernel, jax.ShapeDtypeStruct((4, 128, BLK), BF), parts, [in_vmem] * 8, traffic=3 << 20)


def is_left(owners, mp, dp):
    left = owners[mp, 0] == dp
    for b in range(1, 8):
        left = jnp.logical_or(left, owners[mp, 2 * b] == dp)
    return left


def pick_roots(owners, own_root, other_root):
    def kernel(owners, own, other, lrows, rroot):
        dp, mp, _, _, c, _, _ = place()
        left = is_left(owners, mp, dp)

        def put(lref, rref):
            for h in range(2):
                lrows[h * 256 : h * 256 + 256] = lref[pl.ds(pl.multiple_of(h * 512 + c * 256, 256), 256), :]
            rroot[...] = rref[...]

        @pl.when(left)
        def _():
            put(own, other)

        @pl.when(jnp.logical_not(left))
        def _():
            put(other, own)

    return call(
        kernel,
        (jax.ShapeDtypeStruct((512, BLK), BF), jax.ShapeDtypeStruct((BLK, BLK), BF)),
        (owners, own_root, other_root),
        [in_smem] + [in_vmem] * 2,
        traffic=7 << 20,
    )


def precondition(mine, theirs, lrows, rroot):
    def kernel(mine, theirs, lrows, rroot, grad, out):
        _, _, _, x, c, _, _ = place()
        for side, ref in enumerate((mine, theirs)):
            for dx in range(4):
                for q in range(4):
                    grad[q, (x + dx) & 3, c ^ side] = ref[dx, q * 32 : q * 32 + 32]
        product = jnp.dot(lrows[...], grad[...].reshape(BLK, BLK), preferred_element_type=F32).astype(BF)
        result = jnp.dot(product, rroot[...], preferred_element_type=F32).astype(BF)
        for p in range(8):
            at = (p % 2) * 256 + p // 2 * 64
            out[p] = result[at : at + 64]

    return call(
        kernel,
        (jax.ShapeDtypeStruct((4, 4, 2, 32, BLK), BF), jax.ShapeDtypeStruct((8, 64, BLK), BF)),
        (mine, theirs, lrows, rroot),
        [in_vmem] * 4,
        flops=2 << 30,
        traffic=10 << 20,
    )


def update_statistics(owners, grad, statistics, token):
    def kernel(owners, grad, old, token, out):
        dp, mp = lax.axis_index("dp"), lax.axis_index("mp")
        left = is_left(owners, mp, dp)
        i = pl.program_id(0)
        part = pl.ds(pl.multiple_of(i * 256, 256), 256)

        def store(gram):
            out[...] = 0.9 * old[...] + (1.0 - 0.9) / BLK * gram

        @pl.when(left)
        def _():
            store(lax.dot_general(grad[part, :], grad[...], (((1,), (1,)), ((), ())), preferred_element_type=F32))

        @pl.when(jnp.logical_not(left))
        def _():
            store(lax.dot_general(grad[:, part], grad[...], (((0,), (0,)), ((), ())), preferred_element_type=F32))

    tile = pl.BlockSpec((256, BLK), lambda i: (i, 0))
    return pl.pallas_call(
        kernel,
        grid=(4,),
        out_shape=jax.ShapeDtypeStruct((BLK, BLK), F32),
        in_specs=[in_smem, pl.BlockSpec((BLK, BLK), lambda i: (0, 0)), tile, anywhere],
        out_specs=tile,
        compiler_params=pltpu.CompilerParams(vmem_limit_bytes=VMEM_LIMIT),
        cost_estimate=pl.CostEstimate(flops=2 << 30, bytes_accessed=10 << 20, transcendentals=0),
    )(owners, grad, statistics, token)


def by_rows(owners, spread):
    def kernel(owners, spread, *outs):
        _, mp, yh, x, _, _, _ = place()
        for k in range(4):
            r = (yh ^ (k >> 1)) * 2 + ((x >> 1) ^ (k & 1))
            for j in range(2):
                outs[k][j] = spread[owners[mp, r * 4 + j * 2] >> 1]

    return call(
        kernel,
        (jax.ShapeDtypeStruct((2, 64, BLK), BF),) * 4,
        (owners, spread),
        [in_smem, in_vmem],
        traffic=2 << 20,
    )


def assemble(own, got):
    def kernel(own, g1, g2, g3, out):
        _, _, yh, x, _, _, _ = place()
        mine = yh * 2 + (x >> 1)
        for k, ref in enumerate((own, g1, g2, g3)):
            part = pl.ds(pl.multiple_of((mine ^ k) * 64, 64), 64)
            out[part, :BLK] = ref[0]
            out[part, BLK:] = ref[1]

    return call(
        kernel, jax.ShapeDtypeStruct((256, 2 * BLK), BF), (own, *got), [in_vmem] * 4, traffic=2 << 20
    )


CHIPS = [[p * 2 + c for p in range(8)] for c in range(2)]


FP = 6
FT = 0
T1 = 0
NT = 3
FA = 40 << 30
FO = 20 << 30


def on_device(activations, output_grads, owners, statistics, inv_roots):
    chunks, pieces = gather(activations, output_grads)
    far_other = dp_move(pieces[-1], 0, 0, 1)
    if FA:
        chunks[-1] = (after(chunks[-1][0], cost=FA),) + chunks[-1][1:]
    if FO:
        far_other = after(far_other, cost=FO)
    own_root = copied(inv_roots[0, 0], chunks[-2][0])
    other_root = dp_move(own_root, 0, 0, 1)
    partials = list(block_sums(owners, chunks, pieces + [far_other]))
    partials[FP] = after(partials[FP], other_root)
    lrows, rroot = pick_roots(owners, own_root, other_root)

    parts = [None] * 8
    for dy, dx in ((1, 2), (0, 2), (1, 1), (1, 3), (0, 1), (0, 3), (1, 0), (0, 0)):
        part = partials[dy * 4 + dx]
        parts[dy * 4 + (-dx & 3)] = dp_move(part, dy, dx, 0) if dy or dx else part
    mine = add(parts)
    grad, pieces = precondition(mine, dp_move(mine, 0, 0, 1), lrows, rroot)
    spread = lax.all_to_all(pieces, "dp", 0, 0, axis_index_groups=CHIPS, tiled=True)
    new_stat = update_statistics(owners, grad.reshape(BLK, BLK), statistics[0, 0], spread)
    placed = by_rows(owners, spread)
    got = [dp_move(placed[k], k >> 1, (k & 1) * 2, 0) for k in range(1, 4)]
    return new_stat[None, None], assemble(placed[0], got)


def solution(mesh):
    in_specs = (P("dp", "mp"), P("dp", "mp"), P(), P("mp", "dp", None, None), P("mp", "dp", None, None))
    out_specs = (P("mp", "dp", None, None), P("dp", "mp"))
    return jax.shard_map(on_device, mesh=mesh, in_specs=in_specs, out_specs=out_specs, check_vma=False)
```

profile of v0, /device:TPU:2, one launch (start us, length us, event | category | flops | bytes accessed | tf_op | source)
XLA Modules:
  0.0 143.7 jit_solution(10709757993585121117)
XLA Ops:
  0.7 0.9 copy-done.4
  1.7 1.6 %collective-permute-start = (bf16[64,256]{1,0:T(8,128)(2,1)S(1)}, bf16[64,256]{1,0:T(8,128)(2,1)S(1)}, u32[]{:S(2)}, u32[]{:S(2)}) collective-permute-start(bf16[64,256]{1,0:T(8,128)(2,1)S(1)} %get-tuple-element.31), channel_id=1, source_target_pairs={{0,32},{16,48},{32,64},{48,80},{64,96},{80,112},{96,0},{112,16},{1... | collective-permute-start | bytes 98312 | tf_op jit(solution)/shard_map/ppermute | solution.py:39
  3.3 0.9 collective-permute-start.1
  4.2 2.0 %collective-permute-start.2 = (bf16[64,256]{1,0:T(8,128)(2,1)S(1)}, bf16[64,256]{1,0:T(8,128)(2,1)S(1)}, u32[]{:S(2)}, u32[]{:S(2)}) collective-permute-start(bf16[64,256]{1,0:T(8,128)(2,1)S(1)} %get-tuple-element.33), channel_id=1, source_target_pairs={{0,64},{16,80},{32,96},{48,112},{64,0},{80,16},{96,32},{112,48},{1... | collective-permute-start | bytes 98312 | tf_op jit(solution)/shard_map/ppermute | solution.py:39
  6.2 1.1 collective-permute-done.1.c
  7.2 2.4 %collective-permute-done.2.d = bf16[64,256]{1,0:T(8,128)(2,1)S(1)} collective-permute-done((bf16[64,256]{1,0:T(8,128)(2,1)S(1)}, bf16[64,256]{1,0:T(8,128)(2,1)S(1)}, u32[]{:S(2)}, u32[]{:S(2)}) %collective-permute-start.2) | collective-permute-done | bytes 32800 | tf_op jit(solution)/shard_map/ppermute | solution.py:39
  9.6 1.2 copy-done.2
  10.9 1.2 collective-permute-start.17
  12.6 1.0 collective-permute-done.3.other
  13.7 1.9 %collective-permute-start.6 = (bf16[64,2048]{1,0:T(8,128)(2,1)S(1)}, bf16[64,2048]{1,0:T(8,128)(2,1)S(1)}, u32[]{:S(2)}, u32[]{:S(2)}) collective-permute-start(bf16[64,2048]{1,0:T(8,128)(2,1)S(1)} %shard_map.72), channel_id=1, source_target_pairs={{0,1},{1,2},{2,3},{3,4},{4,5},{5,6},{6,7},{7,0},{8,9},{9,10},{10,1... | collective-permute-start | bytes 786440 | tf_op jit(solution)/shard_map/ppermute | solution.py:66
  15.6 8.3 %collective-permute-done.6.refs_0_ = bf16[64,2048]{1,0:T(8,128)(2,1)S(1)} collective-permute-done((bf16[64,2048]{1,0:T(8,128)(2,1)S(1)}, bf16[64,2048]{1,0:T(8,128)(2,1)S(1)}, u32[]{:S(2)}, u32[]{:S(2)}) %collective-permute-start.6) | collective-permute-done | bytes 262176 | tf_op jit(solution)/shard_map/ppermute | solution.py:66
  24.0 1.3 collective-permute-start.18
  25.3 6.3 %collective-permute-done.9.refs_0_ = bf16[64,2048]{1,0:T(8,128)(2,1)S(1)} collective-permute-done((bf16[64,2048]{1,0:T(8,128)(2,1)S(1)}, bf16[64,2048]{1,0:T(8,128)(2,1)S(1)}, u32[]{:S(2)}, u32[]{:S(2)}) %collective-permute-start.9) | collective-permute-done | bytes 262176 | tf_op jit(solution)/shard_map/ppermute | solution.py:66
  31.7 1.3 collective-permute-start.20
  32.9 1.0 collective-permute-start.10
  34.3 1.7 %collective-permute-start.8 = (bf16[2,32,2048]{2,1,0:T(8,128)(2,1)S(1)}, bf16[2,32,2048]{2,1,0:T(8,128)(2,1)S(1)}, u32[]{:S(2)}, u32[]{:S(2)}) collective-permute-start(bf16[2,32,2048]{2,1,0:T(8,128)(2,1)S(1)} %pad_maximum_fusion), channel_id=1, source_target_pairs={{0,8},{1,9},{2,10},{3,11},{4,12},{5,13},{6,14},{7,15},{8,0},{9,1},... | collective-permute-start | bytes 786440 | tf_op jit(solution)/shard_map/ppermute | solution.py:44
  36.0 4.5 %collective-permute-done.12.refs_0_ = bf16[64,2048]{1,0:T(8,128)(2,1)S(1)} collective-permute-done((bf16[64,2048]{1,0:T(8,128)(2,1)S(1)}, bf16[64,2048]{1,0:T(8,128)(2,1)S(1)}, u32[]{:S(2)}, u32[]{:S(2)}) %collective-permute-start.12) | collective-permute-done | bytes 262176 | tf_op jit(solution)/shard_map/ppermute | solution.py:66
  40.5 1.6 %collective-permute-start.4 = (bf16[32,2048]{1,0:T(8,128)(2,1)S(1)}, bf16[32,2048]{1,0:T(8,128)(2,1)S(1)}, u32[]{:S(2)}, u32[]{:S(2)}) collective-permute-start(bf16[32,2048]{1,0:T(8,128)(2,1)S(1)} %get-tuple-element.34), channel_id=1, source_target_pairs={{0,8},{1,9},{2,10},{3,11},{4,12},{5,13},{6,14},{7,15},{8,0},{9,1},... | collective-permute-start | bytes 393224 | tf_op jit(solution)/shard_map/ppermute | solution.py:44
  42.3 0.5 collective-permute-start.11
  42.9 0.6 collective-permute-done.8.refs_1_.refs_4_
  43.5 0.9 collective-permute-start.15
  44.5 1.3 collective-permute-start.16
  45.8 6.5 %collective-permute-done.16 = bf16[32,2048]{1,0:T(8,128)(2,1)S(1)} collective-permute-done((bf16[32,2048]{1,0:T(8,128)(2,1)S(1)}, bf16[32,2048]{1,0:T(8,128)(2,1)S(1)}, u32[]{:S(2)}, u32[]{:S(2)}) %collective-permute-start.16) | collective-permute-done | bytes 131104 | tf_op jit(solution)/shard_map/ppermute | solution.py:66
  52.8 1.0 collective-permute-start.14
  53.8 0.6 copy-done.1
  54.5 3.4 %collective-permute-done.21.refs_0_ = bf16[256,2048]{1,0:T(8,128)(2,1)S(1)} collective-permute-done((bf16[256,2048]{1,0:T(8,128)(2,1)S(1)}, bf16[256,2048]{1,0:T(8,128)(2,1)S(1)}, u32[]{:S(2)}, u32[]{:S(2)}) %collective-permute-start.21) | collective-permute-done | bytes 1048608 | tf_op jit(solution)/shard_map/ppermute | solution.py:39
  58.2 2.9 %collective-permute-done.14.refs_10_ = bf16[2,32,2048]{2,1,0:T(8,128)(2,1)S(1)} collective-permute-done((bf16[2,32,2048]{2,1,0:T(8,128)(2,1)S(1)}, bf16[2,32,2048]{2,1,0:T(8,128)(2,1)S(1)}, u32[]{:S(2)}, u32[]{:S(2)}) %collective-permute-start.14) | collective-permute-done | bytes 262176 | tf_op jit(solution)/shard_map/ppermute | solution.py:44
  61.1 6.9 %shard_map.84 = (bf16[128,1024]{1,0:T(8,128)(2,1)S(1)}, bf16[128,1024]{1,0:T(8,128)(2,1)S(1)}, bf16[128,1024]{1,0:T(8,128)(2,1)S(1)}, bf16[128,1024]{1,0:T(8,128...) custom-call(s32[16,16]{1,0:T(8,128)S(1)} %copy-done.5, ...), custom_call_target="tpu_custom_call" | custom-call | flops 4294967296 | bytes 8388608 | tf_op jit(solution)/shard_map/pallas_call | solution.py:19
  68.0 1.6 %collective-permute-start.22 = (bf16[128,1024]{1,0:T(8,128)(2,1)S(1)}, bf16[128,1024]{1,0:T(8,128)(2,1)S(1)}, u32[]{:S(2)}, u32[]{:S(2)}) collective-permute-start(bf16[128,1024]{1,0:T(8,128)(2,1)S(1)} %get-tuple-element.43), channel_id=1, source_target_pairs={{0,96},{16,112},{32,0},{48,16},{64,32},{80,48},{96,64},{112,80},{1... | collective-permute-start | bytes 786440 | tf_op jit(solution)/shard_map/ppermute | solution.py:39
  69.6 1.6 %collective-permute-start.23 = (bf16[128,1024]{1,0:T(8,128)(2,1)S(1)}, bf16[128,1024]{1,0:T(8,128)(2,1)S(1)}, u32[]{:S(2)}, u32[]{:S(2)}) collective-permute-start(bf16[128,1024]{1,0:T(8,128)(2,1)S(1)} %get-tuple-element.44), channel_id=1, source_target_pairs={{0,64},{16,80},{32,96},{48,112},{64,0},{80,16},{96,32},{112,48},{1... | collective-permute-start | bytes 786440 | tf_op jit(solution)/shard_map/ppermute | solution.py:39
  71.2 2.0 %collective-permute-start.24 = (bf16[128,1024]{1,0:T(8,128)(2,1)S(1)}, bf16[128,1024]{1,0:T(8,128)(2,1)S(1)}, u32[]{:S(2)}, u32[]{:S(2)}) collective-permute-start(bf16[128,1024]{1,0:T(8,128)(2,1)S(1)} %get-tuple-element.45), channel_id=1, source_target_pairs={{0,32},{16,48},{32,64},{48,80},{64,96},{80,112},{96,0},{112,16},{1... | collective-permute-start | bytes 786440 | tf_op jit(solution)/shard_map/ppermute | solution.py:39
  73.2 2.9 %collective-permute-start.25 = (bf16[128,1024]{1,0:T(8,128)(2,1)S(1)}, bf16[128,1024]{1,0:T(8,128)(2,1)S(1)}, u32[]{:S(2)}, u32[]{:S(2)}) collective-permute-start(bf16[128,1024]{1,0:T(8,128)(2,1)S(1)} %get-tuple-element.46), channel_id=1, source_target_pairs={{0,128},{16,144},{32,160},{48,176},{64,192},{80,208},{96,224},{112... | collective-permute-start | bytes 786440 | tf_op jit(solution)/shard_map/ppermute | solution.py:39
  76.3 5.0 %collective-permute-start.29 = (bf16[128,1024]{1,0:T(8,128)(2,1)S(1)}, bf16[128,1024]{1,0:T(8,128)(2,1)S(1)}, u32[]{:S(2)}, u32[]{:S(2)}) collective-permute-start(bf16[128,1024]{1,0:T(8,128)(2,1)S(1)} %get-tuple-element.49), channel_id=1, source_target_pairs={{0,160},{16,176},{32,192},{48,208},{64,224},{80,240},{96,128},{112... | collective-permute-start | bytes 786440 | tf_op jit(solution)/shard_map/ppermute | solution.py:39
  81.3 2.8 %collective-permute-done.23.refs_2_ = bf16[128,1024]{1,0:T(8,128)(2,1)S(1)} collective-permute-done((bf16[128,1024]{1,0:T(8,128)(2,1)S(1)}, bf16[128,1024]{1,0:T(8,128)(2,1)S(1)}, u32[]{:S(2)}, u32[]{:S(2)}) %collective-permute-start.23) | collective-permute-done | bytes 262176 | tf_op jit(solution)/shard_map/ppermute | solution.py:39
  84.1 4.3 %collective-permute-start.28 = (bf16[128,1024]{1,0:T(8,128)(2,1)S(1)}, bf16[128,1024]{1,0:T(8,128)(2,1)S(1)}, u32[]{:S(2)}, u32[]{:S(2)}) collective-permute-start(bf16[128,1024]{1,0:T(8,128)(2,1)S(1)} %shard_map.86), channel_id=1, source_target_pairs={{0,192},{16,208},{32,224},{48,240},{64,128},{80,144},{96,160},{112... | collective-permute-start | bytes 786440 | tf_op jit(solution)/shard_map/ppermute | solution.py:39
  88.3 8.7 %collective-permute-done.25.refs_4_ = bf16[128,1024]{1,0:T(8,128)(2,1)S(1)} collective-permute-done((bf16[128,1024]{1,0:T(8,128)(2,1)S(1)}, bf16[128,1024]{1,0:T(8,128)(2,1)S(1)}, u32[]{:S(2)}, u32[]{:S(2)}) %collective-permute-start.25) | collective-permute-done | bytes 262176 | tf_op jit(solution)/shard_map/ppermute | solution.py:39
  97.1 2.1 %collective-permute-done.28.refs_6_ = bf16[128,1024]{1,0:T(8,128)(2,1)S(1)} collective-permute-done((bf16[128,1024]{1,0:T(8,128)(2,1)S(1)}, bf16[128,1024]{1,0:T(8,128)(2,1)S(1)}, u32[]{:S(2)}, u32[]{:S(2)}) %collective-permute-start.28) | collective-permute-done | bytes 262176 | tf_op jit(solution)/shard_map/ppermute | solution.py:39
  99.5 1.1 shard_map.88
  100.6 1.5 %collective-permute-done.30.theirs = bf16[4,128,1024]{2,1,0:T(8,128)(2,1)S(1)} collective-permute-done((bf16[4,128,1024]{2,1,0:T(8,128)(2,1)S(1)}, bf16[4,128,1024]{2,1,0:T(8,128)(2,1)S(1)}, u32[]{:S(2)}, u32[]{:S(2)}) %collective-permute-start.30) | collective-permute-done | bytes 1048608 | tf_op jit(solution)/shard_map/ppermute | solution.py:39
  102.2 2.5 %shard_map.89 = (bf16[4,4,2,32,1024]{4,3,2,1,0:T(8,128)(2,1)S(1)}, bf16[8,64,1024]{2,1,0:T(8,128)(2,1)S(1)}) custom-call(bf16[4,128,1024]{2,1,0:T(8,128)(2,1)S(1)} %shard_map.87.mine, bf16[4,128,1024]{2,1,0:T(8,128)(2,1)S(1)} %collective-permute-done.30.theirs, bf16[512,1024]{1,0:T(8,128)(2,1)S(1)} %get-tuple-element.50.lrows, ...), custom_call_target="tpu_custom_call" | custom-call | flops 2147483648 | bytes 10485760 | tf_op jit(solution)/shard_map/pallas_call | solution.py:19
  104.7 22.5 %all_to_all.5.token.spread = bf16[8,64,1024]{2,1,0:T(8,128)(2,1)S(1)} all-to-all(bf16[8,64,1024]{2,1,0:T(8,128)(2,1)S(1)} %get-tuple-element.53), channel_id=1, replica_groups={{0,32,64,96,128,160,192,224},{16,48,80,112,144,176,208,240},{1,33,65,97..., dimensions={0} | all-to-all | bytes 2097152 | tf_op jit(solution)/shard_map/all_to_all | solution.py:408
  127.1 0.8 shard_map.91
  127.9 1.2 collective-permute-start.31
  129.1 0.9 collective-permute-start.32
  130.0 4.5 %collective-permute-start.33 = (bf16[2,64,1024]{2,1,0:T(8,128)(2,1)S(1)}, bf16[2,64,1024]{2,1,0:T(8,128)(2,1)S(1)}, u32[]{:S(2)}, u32[]{:S(2)}) collective-permute-start(bf16[2,64,1024]{2,1,0:T(8,128)(2,1)S(1)} %get-tuple-element.57), channel_id=1, source_target_pairs={{0,192},{16,208},{32,224},{48,240},{64,128},{80,144},{96,160},{112... | collective-permute-start | bytes 786440 | tf_op jit(solution)/shard_map/ppermute | solution.py:39
  134.5 5.0 %shard_map.90 = f32[1024,1024]{1,0:T(8,128)} custom-call(s32[16,16]{1,0:T(8,128)S(1)} %copy-done.5, bf16[1024,1024]{1,0:T(8,128)(2,1)S(1)} %bitcast.14, f32[1024,1024]{1,0:T(8,128)S(1)} %bitcast.13, bf16[8,64,1024]{2,1,0:T(8,128)(2,1)S(1)} %all_to_all.5.token.spread), custom_call_target="tpu_custom_call" | custom-call | flops 2147483648 | bytes 10485760 | tf_op jit(solution)/shard_map/pallas_call | solution.py:336
  139.5 3.1 %collective-permute-done.32.g2 = bf16[2,64,1024]{2,1,0:T(8,128)(2,1)S(1)} collective-permute-done((bf16[2,64,1024]{2,1,0:T(8,128)(2,1)S(1)}, bf16[2,64,1024]{2,1,0:T(8,128)(2,1)S(1)}, u32[]{:S(2)}, u32[]{:S(2)}) %collective-permute-start.32) | collective-permute-done | bytes 262176 | tf_op jit(solution)/shard_map/ppermute | solution.py:39
  142.6 1.1 shard_map.92
  (62 shorter events, 3.2 us)
Async XLA Ops:
  0.6 13.0 %collective-permute-start.5 = (bf16[256,2048]{1,0:T(8,128)(2,1)}, bf16[256,2048]{1,0:T(8,128)(2,1)S(1)}, u32[]{:S(2)}, u32[]{:S(2)}) collective-permute-start(bf16[256,2048]{1,0:T(8,128)(2,1)} %refs_13_.1), channel_id=1, source_target_pairs={{0,16},{16,0},{32,48},{48,32},{64,80},{80,64},{96,112},{112,96},{1... | collective-permute-start | bytes 3145736 | tf_op jit(solution)/shard_map/ppermute | solution.py:39
  0.7 0.9 copy-start.4
  1.7 4.4 %collective-permute-start = (bf16[64,256]{1,0:T(8,128)(2,1)S(1)}, bf16[64,256]{1,0:T(8,128)(2,1)S(1)}, u32[]{:S(2)}, u32[]{:S(2)}) collective-permute-start(bf16[64,256]{1,0:T(8,128)(2,1)S(1)} %get-tuple-element.31), channel_id=1, source_target_pairs={{0,32},{16,48},{32,64},{48,80},{64,96},{80,112},{96,0},{112,16},{1... | collective-permute-start | bytes 98312 | tf_op jit(solution)/shard_map/ppermute | solution.py:39
  3.3 3.9 %collective-permute-start.1 = (bf16[64,256]{1,0:T(8,128)(2,1)S(1)}, bf16[64,256]{1,0:T(8,128)(2,1)S(1)}, u32[]{:S(2)}, u32[]{:S(2)}) collective-permute-start(bf16[64,256]{1,0:T(8,128)(2,1)S(1)} %get-tuple-element.32), channel_id=1, source_target_pairs={{0,96},{16,112},{32,0},{48,16},{64,32},{80,48},{96,64},{112,80},{1... | collective-permute-start | bytes 98312 | tf_op jit(solution)/shard_map/ppermute | solution.py:39
  4.2 5.4 %collective-permute-start.2 = (bf16[64,256]{1,0:T(8,128)(2,1)S(1)}, bf16[64,256]{1,0:T(8,128)(2,1)S(1)}, u32[]{:S(2)}, u32[]{:S(2)}) collective-permute-start(bf16[64,256]{1,0:T(8,128)(2,1)S(1)} %get-tuple-element.33), channel_id=1, source_target_pairs={{0,64},{16,80},{32,96},{48,112},{64,0},{80,16},{96,32},{112,48},{1... | collective-permute-start | bytes 98312 | tf_op jit(solution)/shard_map/ppermute | solution.py:39
  9.6 1.2 copy-start.2
  10.9 20.7 %collective-permute-start.17 = (bf16[256,2048]{1,0:T(8,128)(2,1)S(1)}, bf16[256,2048]{1,0:T(8,128)(2,1)S(1)}, u32[]{:S(2)}, u32[]{:S(2)}) collective-permute-start(bf16[256,2048]{1,0:T(8,128)(2,1)S(1)} %shard_map.80), channel_id=1, source_target_pairs={{0,32},{1,33},{2,34},{3,35},{4,36},{5,37},{6,38},{7,39},{8,40},{9,... | collective-permute-start | bytes 3145736 | tf_op jit(solution)/shard_map/ppermute | solution.py:66
  12.1 1.5 %collective-permute-start.3 = (bf16[64,1024]{1,0:T(8,128)(2,1)S(1)}, bf16[64,1024]{1,0:T(8,128)(2,1)S(1)}, u32[]{:S(2)}, u32[]{:S(2)}) collective-permute-start(bf16[64,1024]{1,0:T(8,128)(2,1)S(1)} %shard_map.69.half.refs_1_.token), channel_id=1, source_target_pairs={{0,16},{16,0},{32,48},{48,32},{64,80},{80,64},{96,112},{112,96},{1... | collective-permute-start | bytes 393224 | tf_op jit(solution)/shard_map/ppermute | solution.py:39
  13.7 10.2 %collective-permute-start.6 = (bf16[64,2048]{1,0:T(8,128)(2,1)S(1)}, bf16[64,2048]{1,0:T(8,128)(2,1)S(1)}, u32[]{:S(2)}, u32[]{:S(2)}) collective-permute-start(bf16[64,2048]{1,0:T(8,128)(2,1)S(1)} %shard_map.72), channel_id=1, source_target_pairs={{0,1},{1,2},{2,3},{3,4},{4,5},{5,6},{6,7},{7,0},{8,9},{9,10},{10,1... | collective-permute-start | bytes 786440 | tf_op jit(solution)/shard_map/ppermute | solution.py:66
  23.9 7.7 %collective-permute-start.9 = (bf16[64,2048]{1,0:T(8,128)(2,1)S(1)}, bf16[64,2048]{1,0:T(8,128)(2,1)S(1)}, u32[]{:S(2)}, u32[]{:S(2)}) collective-permute-start(bf16[64,2048]{1,0:T(8,128)(2,1)S(1)} %shard_map.74), channel_id=1, source_target_pairs={{0,1},{1,2},{2,3},{3,4},{4,5},{5,6},{6,7},{7,0},{8,9},{9,10},{10,1... | collective-permute-start | bytes 786440 | tf_op jit(solution)/shard_map/ppermute | solution.py:66
  24.0 18.3 %collective-permute-start.18 = (bf16[256,2048]{1,0:T(8,128)(2,1)S(1)}, bf16[256,2048]{1,0:T(8,128)(2,1)S(1)}, u32[]{:S(2)}, u32[]{:S(2)}) collective-permute-start(bf16[256,2048]{1,0:T(8,128)(2,1)S(1)} %shard_map.71.refs_1_.refs_14_), channel_id=1, source_target_pairs={{0,32},{1,33},{2,34},{3,35},{4,36},{5,37},{6,38},{7,39},{8,40},{9,... | collective-permute-start | bytes 3145736 | tf_op jit(solution)/shard_map/ppermute | solution.py:66
  31.7 20.6 %collective-permute-start.20 = (bf16[256,2048]{1,0:T(8,128)(2,1)S(1)}, bf16[256,2048]{1,0:T(8,128)(2,1)S(1)}, u32[]{:S(2)}, u32[]{:S(2)}) collective-permute-start(bf16[256,2048]{1,0:T(8,128)(2,1)S(1)} %shard_map.82), channel_id=1, source_target_pairs={{0,32},{1,33},{2,34},{3,35},{4,36},{5,37},{6,38},{7,39},{8,40},{9,... | collective-permute-start | bytes 3145736 | tf_op jit(solution)/shard_map/ppermute | solution.py:66
  32.9 1.3 collective-permute-start.7
  32.9 7.6 %collective-permute-start.12 = (bf16[64,2048]{1,0:T(8,128)(2,1)S(1)}, bf16[64,2048]{1,0:T(8,128)(2,1)S(1)}, u32[]{:S(2)}, u32[]{:S(2)}) collective-permute-start(bf16[64,2048]{1,0:T(8,128)(2,1)S(1)} %shard_map.76), channel_id=1, source_target_pairs={{0,1},{1,2},{2,3},{3,4},{4,5},{5,6},{6,7},{7,0},{8,9},{9,10},{10,1... | collective-permute-start | bytes 786440 | tf_op jit(solution)/shard_map/ppermute | solution.py:66
  32.9 9.2 %collective-permute-start.10 = (bf16[1,32,2048]{2,1,0:T(8,128)(2,1)S(1)}, bf16[1,32,2048]{2,1,0:T(8,128)(2,1)S(1)}, u32[]{:S(2)}, u32[]{:S(2)}) collective-permute-start(bf16[1,32,2048]{2,1,0:T(8,128)(2,1)S(1)} %get-tuple-element.39), channel_id=1, source_target_pairs={{0,16},{16,0},{32,48},{48,32},{64,80},{80,64},{96,112},{112,96},{1... | collective-permute-start | bytes 393224 | tf_op jit(solution)/shard_map/ppermute | solution.py:39
  34.3 9.2 %collective-permute-start.8 = (bf16[2,32,2048]{2,1,0:T(8,128)(2,1)S(1)}, bf16[2,32,2048]{2,1,0:T(8,128)(2,1)S(1)}, u32[]{:S(2)}, u32[]{:S(2)}) collective-permute-start(bf16[2,32,2048]{2,1,0:T(8,128)(2,1)S(1)} %pad_maximum_fusion), channel_id=1, source_target_pairs={{0,8},{1,9},{2,10},{3,11},{4,12},{5,13},{6,14},{7,15},{8,0},{9,1},... | collective-permute-start | bytes 786440 | tf_op jit(solution)/shard_map/ppermute | solution.py:44
  40.5 17.7 %collective-permute-start.4 = (bf16[32,2048]{1,0:T(8,128)(2,1)S(1)}, bf16[32,2048]{1,0:T(8,128)(2,1)S(1)}, u32[]{:S(2)}, u32[]{:S(2)}) collective-permute-start(bf16[32,2048]{1,0:T(8,128)(2,1)S(1)} %get-tuple-element.34), channel_id=1, source_target_pairs={{0,8},{1,9},{2,10},{3,11},{4,12},{5,13},{6,14},{7,15},{8,0},{9,1},... | collective-permute-start | bytes 393224 | tf_op jit(solution)/shard_map/ppermute | solution.py:44
  42.1 2.4 %collective-permute-start.13 = (bf16[1,32,2048]{2,1,0:T(8,128)(2,1)S(1)}, bf16[1,32,2048]{2,1,0:T(8,128)(2,1)S(1)}, u32[]{:S(2)}, u32[]{:S(2)}) collective-permute-start(bf16[1,32,2048]{2,1,0:T(8,128)(2,1)S(1)} %get-tuple-element.41), channel_id=1, source_target_pairs={{0,16},{16,0},{32,48},{48,32},{64,80},{80,64},{96,112},{112,96},{1... | collective-permute-start | bytes 393224 | tf_op jit(solution)/shard_map/ppermute | solution.py:39
  42.3 15.9 %collective-permute-start.11 = (bf16[2,32,2048]{2,1,0:T(8,128)(2,1)S(1)}, bf16[2,32,2048]{2,1,0:T(8,128)(2,1)S(1)}, u32[]{:S(2)}, u32[]{:S(2)}) collective-permute-start(bf16[2,32,2048]{2,1,0:T(8,128)(2,1)S(1)} %pad_maximum_fusion.1), channel_id=1, source_target_pairs={{0,8},{1,9},{2,10},{3,11},{4,12},{5,13},{6,14},{7,15},{8,0},{9,1},... | collective-permute-start | bytes 786440 | tf_op jit(solution)/shard_map/ppermute | solution.py:44
  43.5 9.2 %collective-permute-start.15 = (bf16[32,2048]{1,0:T(8,128)(2,1)S(1)}, bf16[32,2048]{1,0:T(8,128)(2,1)S(1)}, u32[]{:S(2)}, u32[]{:S(2)}) collective-permute-start(bf16[32,2048]{1,0:T(8,128)(2,1)S(1)} %bitcast.16), channel_id=1, source_target_pairs={{0,1},{1,2},{2,3},{3,4},{4,5},{5,6},{6,7},{7,0},{8,9},{9,10},{10,1... | collective-permute-start | bytes 393224 | tf_op jit(solution)/shard_map/ppermute | solution.py:66
  44.5 7.8 %collective-permute-start.16 = (bf16[32,2048]{1,0:T(8,128)(2,1)S(1)}, bf16[32,2048]{1,0:T(8,128)(2,1)S(1)}, u32[]{:S(2)}, u32[]{:S(2)}) collective-permute-start(bf16[32,2048]{1,0:T(8,128)(2,1)S(1)} %bitcast.17), channel_id=1, source_target_pairs={{0,9},{1,10},{2,11},{3,12},{4,13},{5,14},{6,15},{7,8},{8,1},{9,2},... | collective-permute-start | bytes 393224 | tf_op jit(solution)/shard_map/ppermute | solution.py:66
  52.3 5.8 %collective-permute-start.19 = (bf16[2,256,2048]{2,1,0:T(8,128)(2,1)S(1)}, bf16[2,256,2048]{2,1,0:T(8,128)(2,1)S(1)}, u32[]{:S(2)}, u32[]{:S(2)}) collective-permute-start(bf16[2,256,2048]{2,1,0:T(8,128)(2,1)S(1)} %shard_map.81), channel_id=1, source_target_pairs={{0,16},{16,0},{32,48},{48,32},{64,80},{80,64},{96,112},{112,96},{1... | collective-permute-start | bytes 6291464 | tf_op jit(solution)/shard_map/ppermute | solution.py:39
  52.3 5.7 %collective-permute-start.21 = (bf16[256,2048]{1,0:T(8,128)(2,1)S(1)}, bf16[256,2048]{1,0:T(8,128)(2,1)S(1)}, u32[]{:S(2)}, u32[]{:S(2)}) collective-permute-start(bf16[256,2048]{1,0:T(8,128)(2,1)S(1)} %collective-permute-done.20.refs_19_), channel_id=1, source_target_pairs={{0,16},{16,0},{32,48},{48,32},{64,80},{80,64},{96,112},{112,96},{1... | collective-permute-start | bytes 3145736 | tf_op jit(solution)/shard_map/ppermute | solution.py:39
  52.8 1.6 %copy-start.1 = (bf16[1,1,1024,1024]{3,2,1,0:T(8,128)(2,1)S(1)}, bf16[1,1,1024,1024]{3,2,1,0:T(8,128)(2,1)}, u32[]{:S(2)}) copy-start(bf16[1,1,1024,1024]{3,2,1,0:T(8,128)(2,1)} %param.9) | copy-start | bytes 6291460
  52.8 8.3 %collective-permute-start.14 = (bf16[2,32,2048]{2,1,0:T(8,128)(2,1)S(1)}, bf16[2,32,2048]{2,1,0:T(8,128)(2,1)S(1)}, u32[]{:S(2)}, u32[]{:S(2)}) collective-permute-start(bf16[2,32,2048]{2,1,0:T(8,128)(2,1)S(1)} %pad_maximum_fusion.2), channel_id=1, source_target_pairs={{0,8},{1,9},{2,10},{3,11},{4,12},{5,13},{6,14},{7,15},{8,0},{9,1},... | collective-permute-start | bytes 786440 | tf_op jit(solution)/shard_map/ppermute | solution.py:44
  57.9 18.1 %collective-permute-start.27 = (bf16[1024,1024]{1,0:T(8,128)(2,1)S(1)}, bf16[1024,1024]{1,0:T(8,128)(2,1)S(1)}, u32[]{:S(2)}, u32[]{:S(2)}) collective-permute-start(bf16[1024,1024]{1,0:T(8,128)(2,1)S(1)} %shard_map.85.own), channel_id=1, source_target_pairs={{0,16},{16,0},{32,48},{48,32},{64,80},{80,64},{96,112},{112,96},{1... | collective-permute-start | bytes 6291464 | tf_op jit(solution)/shard_map/ppermute | solution.py:39
  58.1 3.0 %copy-start.3 = (bf16[256,2048]{1,0:T(8,128)(2,1)S(1)}, bf16[256,2048]{1,0:T(8,128)(2,1)}, u32[]{:S(2)}) copy-start(bf16[256,2048]{1,0:T(8,128)(2,1)} %refs_13_.1) | copy-start | bytes 3145732
  58.1 3.0 %copy-start.5 = (s32[16,16]{1,0:T(8,128)S(1)}, s32[16,16]{1,0:T(8,128)}, u32[]{:S(2)}) copy-start(s32[16,16]{1,0:T(8,128)} %owners.7) | copy-start | bytes 3076
  68.0 8.3 %collective-permute-start.22 = (bf16[128,1024]{1,0:T(8,128)(2,1)S(1)}, bf16[128,1024]{1,0:T(8,128)(2,1)S(1)}, u32[]{:S(2)}, u32[]{:S(2)}) collective-permute-start(bf16[128,1024]{1,0:T(8,128)(2,1)S(1)} %get-tuple-element.43), channel_id=1, source_target_pairs={{0,96},{16,112},{32,0},{48,16},{64,32},{80,48},{96,64},{112,80},{1... | collective-permute-start | bytes 786440 | tf_op jit(solution)/shard_map/ppermute | solution.py:39
  69.6 14.5 %collective-permute-start.23 = (bf16[128,1024]{1,0:T(8,128)(2,1)S(1)}, bf16[128,1024]{1,0:T(8,128)(2,1)S(1)}, u32[]{:S(2)}, u32[]{:S(2)}) collective-permute-start(bf16[128,1024]{1,0:T(8,128)(2,1)S(1)} %get-tuple-element.44), channel_id=1, source_target_pairs={{0,64},{16,80},{32,96},{48,112},{64,0},{80,16},{96,32},{112,48},{1... | collective-permute-start | bytes 786440 | tf_op jit(solution)/shard_map/ppermute | solution.py:39
  71.2 17.1 %collective-permute-start.24 = (bf16[128,1024]{1,0:T(8,128)(2,1)S(1)}, bf16[128,1024]{1,0:T(8,128)(2,1)S(1)}, u32[]{:S(2)}, u32[]{:S(2)}) collective-permute-start(bf16[128,1024]{1,0:T(8,128)(2,1)S(1)} %get-tuple-element.45), channel_id=1, source_target_pairs={{0,32},{16,48},{32,64},{48,80},{64,96},{80,112},{96,0},{112,16},{1... | collective-permute-start | bytes 786440 | tf_op jit(solution)/shard_map/ppermute | solution.py:39
  73.2 23.9 %collective-permute-start.25 = (bf16[128,1024]{1,0:T(8,128)(2,1)S(1)}, bf16[128,1024]{1,0:T(8,128)(2,1)S(1)}, u32[]{:S(2)}, u32[]{:S(2)}) collective-permute-start(bf16[128,1024]{1,0:T(8,128)(2,1)S(1)} %get-tuple-element.46), channel_id=1, source_target_pairs={{0,128},{16,144},{32,160},{48,176},{64,192},{80,208},{96,224},{112... | collective-permute-start | bytes 786440 | tf_op jit(solution)/shard_map/ppermute | solution.py:39
  76.1 21.0 %collective-permute-start.26 = (bf16[128,1024]{1,0:T(8,128)(2,1)S(1)}, bf16[128,1024]{1,0:T(8,128)(2,1)S(1)}, u32[]{:S(2)}, u32[]{:S(2)}) collective-permute-start(bf16[128,1024]{1,0:T(8,128)(2,1)S(1)} %get-tuple-element.47), channel_id=1, source_target_pairs={{0,224},{16,240},{32,128},{48,144},{64,160},{80,176},{96,192},{112... | collective-permute-start | bytes 786440 | tf_op jit(solution)/shard_map/ppermute | solution.py:39
  76.3 20.8 %collective-permute-start.29 = (bf16[128,1024]{1,0:T(8,128)(2,1)S(1)}, bf16[128,1024]{1,0:T(8,128)(2,1)S(1)}, u32[]{:S(2)}, u32[]{:S(2)}) collective-permute-start(bf16[128,1024]{1,0:T(8,128)(2,1)S(1)} %get-tuple-element.49), channel_id=1, source_target_pairs={{0,160},{16,176},{32,192},{48,208},{64,224},{80,240},{96,128},{112... | collective-permute-start | bytes 786440 | tf_op jit(solution)/shard_map/ppermute | solution.py:39
  84.1 15.1 %collective-permute-start.28 = (bf16[128,1024]{1,0:T(8,128)(2,1)S(1)}, bf16[128,1024]{1,0:T(8,128)(2,1)S(1)}, u32[]{:S(2)}, u32[]{:S(2)}) collective-permute-start(bf16[128,1024]{1,0:T(8,128)(2,1)S(1)} %shard_map.86), channel_id=1, source_target_pairs={{0,192},{16,208},{32,224},{48,240},{64,128},{80,144},{96,160},{112... | collective-permute-start | bytes 786440 | tf_op jit(solution)/shard_map/ppermute | solution.py:39
  99.4 2.7 %collective-permute-start.30 = (bf16[4,128,1024]{2,1,0:T(8,128)(2,1)S(1)}, bf16[4,128,1024]{2,1,0:T(8,128)(2,1)S(1)}, u32[]{:S(2)}, u32[]{:S(2)}) collective-permute-start(bf16[4,128,1024]{2,1,0:T(8,128)(2,1)S(1)} %shard_map.87.mine), channel_id=1, source_target_pairs={{0,16},{16,0},{32,48},{48,32},{64,80},{80,64},{96,112},{112,96},{1... | collective-permute-start | bytes 3145736 | tf_op jit(solution)/shard_map/ppermute | solution.py:39
  102.2 32.3 %copy-start = (f32[1,1,1024,1024]{3,2,1,0:T(8,128)S(1)}, f32[1,1,1024,1024]{3,2,1,0:T(8,128)}, u32[]{:S(2)}) copy-start(f32[1,1,1024,1024]{3,2,1,0:T(8,128)} %param.8) | copy-start | bytes 12582916
  127.9 11.6 %collective-permute-start.31 = (bf16[2,64,1024]{2,1,0:T(8,128)(2,1)S(1)}, bf16[2,64,1024]{2,1,0:T(8,128)(2,1)S(1)}, u32[]{:S(2)}, u32[]{:S(2)}) collective-permute-start(bf16[2,64,1024]{2,1,0:T(8,128)(2,1)S(1)} %get-tuple-element.55), channel_id=1, source_target_pairs={{0,64},{16,80},{32,96},{48,112},{64,0},{80,16},{96,32},{112,48},{1... | collective-permute-start | bytes 786440 | tf_op jit(solution)/shard_map/ppermute | solution.py:39
  129.1 13.5 %collective-permute-start.32 = (bf16[2,64,1024]{2,1,0:T(8,128)(2,1)S(1)}, bf16[2,64,1024]{2,1,0:T(8,128)(2,1)S(1)}, u32[]{:S(2)}, u32[]{:S(2)}) collective-permute-start(bf16[2,64,1024]{2,1,0:T(8,128)(2,1)S(1)} %get-tuple-element.56), channel_id=1, source_target_pairs={{0,128},{16,144},{32,160},{48,176},{64,192},{80,208},{96,224},{112... | collective-permute-start | bytes 786440 | tf_op jit(solution)/shard_map/ppermute | solution.py:39
  130.0 12.6 %collective-permute-start.33 = (bf16[2,64,1024]{2,1,0:T(8,128)(2,1)S(1)}, bf16[2,64,1024]{2,1,0:T(8,128)(2,1)S(1)}, u32[]{:S(2)}, u32[]{:S(2)}) collective-permute-start(bf16[2,64,1024]{2,1,0:T(8,128)(2,1)S(1)} %get-tuple-element.57), channel_id=1, source_target_pairs={{0,192},{16,208},{32,224},{48,240},{64,128},{80,144},{96,160},{112... | collective-permute-start | bytes 786440 | tf_op jit(solution)/shard_map/ppermute | solution.py:39
where the time goes:
time: 144 us
  waiting for transfers between devices  55.6 us (39%)
  starting transfers between devices  43.6 us (30%)
  blocking collectives  22.5 us (16%)
  Pallas kernels  18.2 us (13%)
  local copies, waits for them, and re-layouts  2.85 us (2%)
    ppermute x22, starting transfers between devices, dp_move(): return lax.ppermute(v, 'dp', pairs)  30.9 us
    ppermute x22, waiting for transfers between devices, dp_move(): return lax.ppermute(v, 'dp', pairs)  26.5 us
    ppermute x8, waiting for transfers between devices, side_move(): return lax.ppermute(v, ('dp', 'mp'), pairs)  25.6 us
    all_to_all x1, blocking collectives, on_device(): lax.all_to_all(pieces, 'dp', 0, 0, axis_index_groups=CHIPS, tiled=True)  22.5 us
    pallas_call x24, Pallas kernels, call(): pl.pallas_call(kernel, out_shape=outs, in_specs=in_specs, out_specs=kw.po...  13.1 us
    ppermute x8, starting transfers between devices, side_move(): return lax.ppermute(v, ('dp', 'mp'), pairs)  7.93 us
    pallas_call x1, Pallas kernels, update_statistics(): pl.pallas_call(kernel, grid=(4,), out_shape=jax.ShapeDtypeStruct((BLK, BL...  5.01 us
    ppermute x4, starting transfers between devices, mp_move(): return lax.ppermute(v, 'mp', pairs)  4.78 us
  transfers between devices with their start and end apart: 34, of which 17 were waited for; matrix products, arithmetic and copies ran while one was open for 0% of the time, Pallas kernels for 9%

commit v1 on v0

--- a/solution.py
+++ b/solution.py
@@ -145,16 +145,21 @@
     )
 
 
-def swapped(a, b, token):
-    def kernel(a, b, token, out):
-        out[0] = a[...]
-        out[1] = b[...]
-
-    both = call(
-        kernel, jax.ShapeDtypeStruct((2, 256, 2048), BF), (a, b, token), [in_vmem] * 2 + [anywhere], traffic=4 << 20
-    )
-    both = dp_move(both, 0, 0, 1)
-    return both[0], both[1]
+def both_cores(own, other, token):
+    def kernel(own, other, token, out):
+        out[0] = own[...]
+        out[1] = other[...]
+
+    return call(
+        kernel, jax.ShapeDtypeStruct((2, 256, 2048), BF), (own, other, token), [in_vmem] * 2 + [anywhere], traffic=4 << 20
+    )
+
+
+def first_of(value):
+    def kernel(value, out):
+        out[...] = value[0]
+
+    return call(kernel, jax.ShapeDtypeStruct(value.shape[1:], value.dtype), (value,), [in_vmem], traffic=2 << 20)
 
 
 def gather(activations, output_grads):
@@ -164,40 +169,44 @@
     right = dp_move(minus, 0, -1, 0)
     opposite = dp_move(two, 0, 2, 0)
     half = side_by_side((own, left, right, opposite))
-    grads = copied(output_grads, half)
-    own_other = after(own_other, half)
-    near0 = side_move(grads, "x")
-    near1 = side_move(own_other, "x")
+    near = side_move(both_cores(output_grads, own_other, left), "x")
+    far = side_move(first_of(near), "x")
+    near_other = dp_move(near, 0, 0, 1)
 
     chunk, own = by_core(half, dp_move(half, 0, 0, 1))
     own_y = mp_move(own, 1, 0)
+    if CZ:
+        own_y = after(own_y, cost=CZ)
     out = [(own[None], (0,), 0, 0), (own_y[None], (0,), 1, 0)]
-    tokens = {1: (own_other,), 2: (own_other,), 3: (own_other,)}
+    tokens = {1: (own_other,), 2: (own_y,) if CZ else (own_other,), 3: (own_other,)}
     for k in (1, 2, 3):
-        chunk = side_move(after(chunk, *tokens[k]), "z")
+        chunk = side_move(after(chunk, *(tokens[k] if k < 3 or not CG else (first_given,))), "z")
         kept, given = split(chunk)
-        if k == NT:
-            token = kept
         given = dp_move(given, 0, 0, 1)
+        if k == 1 and CG:
+            given = first_given = after(given, cost=CG)
         if k == 3:
-            kept = after(kept, near1, first_y) if T1 else after(kept, first_y)
-        if k == 2:
-            far = side_move(copied(near0, given if FT else kept), "x")
+            kept = after(kept, first_y)
         pair_y = mp_move(jnp.concatenate([kept, given], 0), 1, 0)
+        if k == 1 and CY:
+            pair_y = after(pair_y, cost=CY)
+        if k == 2 and CX:
+            pair_y = after(pair_y, cost=CX)
         out += [(kept, (k,), 0, 0), (given, (k,), 0, 1), (pair_y, (k, -k), 1, 0)]
         if k == 1:
             first_y = pair_y
-    out += [(side_move(kept[0], "z")[None], (4,), 0, 0), (side_move(kept[0], "z", 1)[None], (4,), 1, 0)]
-    return out, [output_grads, own_other, near0, near1, *swapped(near0, near1, token), far]
+    last = side_move(kept[0], "z")
+    out += [(last[None], (4,), 0, 0), (side_move(kept[0], "z", 1)[None], (4,), 1, 0)]
+    return out, [output_grads, own_other, near, near_other, far]
 
 
 def block_sums(owners, chunks, pieces, *tokens):
     n = len(chunks)
 
     def kernel(owners, *refs):
-        own, own_other, near0, near1, near0_other, near1_other, far, far_other = refs[n : n + 8]
-        outs, blocks, feats = refs[-10:-2], refs[-2], refs[-1]
-        _, mp, yh, x, c, yl, z = place()
+        own, own_other, near, near_other, far, far_other = refs[n : n + 6]
+        blocks, feats = refs[-2:]
+        _, mp, _, _, c, yl, z = place()
         for ref, (_, distances, dy, crossed) in zip(refs[:n], chunks):
             for k, dist in enumerate(distances):
                 dz = dist * (2 * (c ^ crossed) - 1)
@@ -206,55 +215,50 @@
         parts = [
             (own, 0, 0),
             (own_other, 0, 1),
-            (near0, 1 + c, 0),
-            (near1, 1 + c, 1),
-            (near0_other, 2 - c, 1),
-            (near1_other, 2 - c, 0),
+            (near.at[0], 1 + c, 0),
+            (near.at[1], 1 + c, 1),
+            (near_other.at[0], 2 - c, 1),
+            (near_other.at[1], 2 - c, 0),
             (far, 3, 0),
             (far_other, 3, 1),
         ]
         for j in range(2):
-            slots = []
-            for r in range(4):
-                pair = owners[mp, (r * 2 + j) * 2] >> 1
-                slots.append(((pair >> 2) ^ yh) * 4 + ((pair - x) & 3))
+            chips = [owners[mp, (r * 2 + j) * 2] >> 1 for r in range(4)]
 
             def step(n, _):
-                total = jnp.zeros((512, 256), F32)
+                cols = pl.ds(pl.multiple_of(n * TN, TN), TN)
+                total = jnp.zeros((512, TN), F32)
                 for ref, k, other in parts:
                     tokens = (c ^ other) * 1024 + k * 256
                     total += jnp.dot(
                         feats[:, pl.ds(pl.multiple_of(tokens, 256), 256)],
-                        ref[:, pl.ds(pl.multiple_of(j * BLK + n * 256, 256), 256)],
+                        ref[:, pl.ds(pl.multiple_of(j * BLK + n * TN, TN), TN)],
                         preferred_element_type=F32,
                     )
                 total = total.astype(BF)
                 for r in range(4):
-                    blocks[slots[r], :, pl.ds(pl.multiple_of(n * 256, 256), 256)] = total[r * 128 : r * 128 + 128]
+                    blocks[chips[r], :, cols] = total[r * 128 : r * 128 + 128]
                 return 0
 
-            lax.fori_loop(0, 4, step, 0)
-        for k in range(8):
-            outs[k][...] = blocks[k]
-
-    return call(
-        kernel,
-        (jax.ShapeDtypeStruct((128, BLK), BF),) * 8,
+            lax.fori_loop(0, BLK // TN, step, 0)
+
+    return call(
+        kernel,
+        jax.ShapeDtypeStruct((8, 128, BLK), BF),
         (owners, *[chunk[0] for chunk in chunks], *pieces, *tokens),
-        [in_smem] + [in_vmem] * (n + 8) + [anywhere] * len(tokens),
-        scratch=[pltpu.VMEM((8, 128, BLK), BF), pltpu.VMEM((512, 2048), BF)],
+        [in_smem] + [in_vmem] * (n + 6) + [anywhere] * len(tokens),
+        scratch=[pltpu.VMEM((512, 2048), BF)],
         flops=4 << 30,
         traffic=8 << 20,
     )
 
 
 def add(parts):
-    def kernel(*refs):
-        out = refs[8]
+    def kernel(parts, out):
         for k in range(4):
-            out[k] = (refs[k][...].astype(F32) + refs[4 + k][...].astype(F32)).astype(BF)
-
-    return call(kernel, jax.ShapeDtypeStruct((4, 128, BLK), BF), parts, [in_vmem] * 8, traffic=3 << 20)
+            out[k] = (parts[k].astype(F32) + parts[4 + k].astype(F32)).astype(BF)
+
+    return call(kernel, jax.ShapeDtypeStruct((4, 128, BLK), BF), (parts,), [in_vmem], traffic=3 << 20)
 
 
 def is_left(owners, mp, dp):
@@ -293,11 +297,11 @@
 
 def precondition(mine, theirs, lrows, rroot):
     def kernel(mine, theirs, lrows, rroot, grad, out):
-        _, _, _, x, c, _, _ = place()
+        c = lax.axis_index("dp") & 1
         for side, ref in enumerate((mine, theirs)):
             for dx in range(4):
                 for q in range(4):
-                    grad[q, (x + dx) & 3, c ^ side] = ref[dx, q * 32 : q * 32 + 32]
+                    grad[q, dx, c ^ side] = ref[dx, q * 32 : q * 32 + 32]
         product = jnp.dot(lrows[...], grad[...].reshape(BLK, BLK), preferred_element_type=F32).astype(BF)
         result = jnp.dot(product, rroot[...], preferred_element_type=F32).astype(BF)
         for p in range(8):
@@ -381,7 +385,13 @@
 FP = 6
 FT = 0
 T1 = 0
-NT = 3
+NT = 4
+TN = 512
+CY = 7 << 30
+CZ = 7 << 30
+CX = 0 << 30
+CG = 7 << 30
+FN = 0 << 30
 FA = 40 << 30
 FO = 20 << 30
 
@@ -395,14 +405,10 @@
         far_other = after(far_other, cost=FO)
     own_root = copied(inv_roots[0, 0], chunks[-2][0])
     other_root = dp_move(own_root, 0, 0, 1)
-    partials = list(block_sums(owners, chunks, pieces + [far_other]))
-    partials[FP] = after(partials[FP], other_root)
+    partials = block_sums(owners, chunks, pieces + [far_other])
+    partials = after(partials, other_root)
     lrows, rroot = pick_roots(owners, own_root, other_root)
-
-    parts = [None] * 8
-    for dy, dx in ((1, 2), (0, 2), (1, 1), (1, 3), (0, 1), (0, 3), (1, 0), (0, 0)):
-        part = partials[dy * 4 + dx]
-        parts[dy * 4 + (-dx & 3)] = dp_move(part, dy, dx, 0) if dy or dx else part
+    parts = lax.all_to_all(partials, "dp", 0, 0, axis_index_groups=CHIPS, tiled=True)
     mine = add(parts)
     grad, pieces = precondition(mine, dp_move(mine, 0, 0, 1), lrows, rroot)
     spread = lax.all_to_all(pieces, "dp", 0, 0, axis_index_groups=CHIPS, tiled=True)

time: 144 us -> 137 us (0.951)
  blocking collectives: 22.5 us -> 54.1 us
  waiting for transfers between devices: 55.6 us -> 34.6 us
  starting transfers between devices: 43.6 us -> 25.4 us
    all_to_all x0 -> x1, blocking collectives: none -> 33.9 us  [on_device(): lax.all_to_all(partials, 'dp', 0, 0, axis_index_groups=CHIPS, tiled=True)]
    ppermute x22 -> x15, waiting for transfers between devices: 26.5 us -> 7.81 us  [dp_move(): return lax.ppermute(v, 'dp', pairs)]
    ppermute x22 -> x15, starting transfers between devices: 30.9 us -> 13 us  [dp_move(): return lax.ppermute(v, 'dp', pairs)]
    all_to_all x1, blocking collectives: 22.5 us -> 20.2 us  [on_device(): lax.all_to_all(pieces, 'dp', 0, 0, axis_index_groups=CHIPS, tiled=True)]
    pallas_call x24 -> x25, Pallas kernels: 13.1 us -> 11.9 us  [call(): pl.pallas_call(kernel, out_shape=outs, in_specs=in_specs, out_specs=kw.po...]
    ppermute x8 -> x7, waiting for transfers between devices: 25.6 us -> 24.7 us  [side_move(): return lax.ppermute(v, ('dp', 'mp'), pairs)]
    ppermute x8 -> x7, starting transfers between devices: 7.93 us -> 8.42 us  [side_move(): return lax.ppermute(v, ('dp', 'mp'), pairs)]
  transfers between devices with their start and end apart: 34 -> 26, of which waited for: 17 -> 11; matrix products, arithmetic and copies ran while one was open for 0% -> 0% of each run, Pallas kernels for 9% -> 9%
where the time goes in v1:
time: 137 us; the launch traced here: 136 us
  blocking collectives  54.1 us (39%)
  waiting for transfers between devices  34.6 us (25%)
  starting transfers between devices  25.4 us (19%)
  Pallas kernels  16.9 us (12%)
  local copies, waits for them, and re-layouts  4.01 us (3%)
    all_to_all x1, blocking collectives, on_device(): lax.all_to_all(partials, 'dp', 0, 0, axis_index_groups=CHIPS, tiled=True)  33.9 us
    ppermute x7, waiting for transfers between devices, side_move(): return lax.ppermute(v, ('dp', 'mp'), pairs)  24.7 us
    all_to_all x1, blocking collectives, on_device(): lax.all_to_all(pieces, 'dp', 0, 0, axis_index_groups=CHIPS, tiled=True)  20.2 us
    ppermute x15, starting transfers between devices, dp_move(): return lax.ppermute(v, 'dp', pairs)  13 us
    pallas_call x25, Pallas kernels, call(): pl.pallas_call(kernel, out_shape=outs, in_specs=in_specs, out_specs=kw.po...  11.9 us
    ppermute x7, starting transfers between devices, side_move(): return lax.ppermute(v, ('dp', 'mp'), pairs)  8.42 us
    ppermute x15, waiting for transfers between devices, dp_move(): return lax.ppermute(v, 'dp', pairs)  7.81 us
    pallas_call x1, Pallas kernels, update_statistics(): pl.pallas_call(kernel, grid=(4,), out_shape=jax.ShapeDtypeStruct((BLK, BL...  5.01 us
  transfers between devices with their start and end apart: 26, of which 11 were waited for; matrix products, arithmetic and copies ran while one was open for 0% of the time, Pallas kernels for 9%

profile of v1, /device:TPU:2, one launch (start us, length us, event | category | flops | bytes accessed | tf_op | source)
XLA Modules:
  0.0 135.9 jit_solution(17065833680984462477)
XLA Ops:
  0.6 0.1 collective-permute-start.5
  0.7 0.9 copy-done.4
  1.6 0.1 shard_map.68
  1.7 1.6 %collective-permute-start = (bf16[64,256]{1,0:T(8,128)(2,1)S(1)}, bf16[64,256]{1,0:T(8,128)(2,1)S(1)}, u32[]{:S(2)}, u32[]{:S(2)}) collective-permute-start(bf16[64,256]{1,0:T(8,128)(2,1)S(1)} %get-tuple-element.23), channel_id=1, source_target_pairs={{0,32},{16,48},{32,64},{48,80},{64,96},{80,112},{96,0},{112,16},{1... | collective-permute-start | bytes 98312 | tf_op jit(solution)/shard_map/ppermute | solution.py:39
  3.3 0.9 collective-permute-start.1
  4.2 2.0 %collective-permute-start.2 = (bf16[64,256]{1,0:T(8,128)(2,1)S(1)}, bf16[64,256]{1,0:T(8,128)(2,1)S(1)}, u32[]{:S(2)}, u32[]{:S(2)}) collective-permute-start(bf16[64,256]{1,0:T(8,128)(2,1)S(1)} %get-tuple-element.25), channel_id=1, source_target_pairs={{0,64},{16,80},{32,96},{48,112},{64,0},{80,16},{96,32},{112,48},{1... | collective-permute-start | bytes 98312 | tf_op jit(solution)/shard_map/ppermute | solution.py:39
  6.2 1.2 copy-done.2
  7.4 0.1 shard_map.82
  7.5 2.7 %collective-permute-start.17 = (bf16[2,256,2048]{2,1,0:T(8,128)(2,1)S(1)}, bf16[2,256,2048]{2,1,0:T(8,128)(2,1)S(1)}, u32[]{:S(2)}, u32[]{:S(2)}) collective-permute-start(bf16[2,256,2048]{2,1,0:T(8,128)(2,1)S(1)} %shard_map.82), channel_id=1, source_target_pairs={{0,32},{1,33},{2,34},{3,35},{4,36},{5,37},{6,38},{7,39},{8,40},{9,... | collective-permute-start | bytes 6291464 | tf_op jit(solution)/shard_map/ppermute | solution.py:66
  10.3 0.1 collective-permute-start.3
  10.4 1.3 collective-permute-done.3.other
  11.7 1.0 collective-permute-start.6
  12.8 1.6 %collective-permute-start.4 = (bf16[32,2048]{1,0:T(8,128)(2,1)S(1)}, bf16[32,2048]{1,0:T(8,128)(2,1)S(1)}, u32[]{:S(2)}, u32[]{:S(2)}) collective-permute-start(bf16[32,2048]{1,0:T(8,128)(2,1)S(1)} %get-tuple-element.26), channel_id=1, source_target_pairs={{0,8},{1,9},{2,10},{3,11},{4,12},{5,13},{6,14},{7,15},{8,0},{9,1},... | collective-permute-start | bytes 393224 | tf_op jit(solution)/shard_map/ppermute | solution.py:44
  14.3 6.7 %collective-permute-done.6.refs_0_ = bf16[64,2048]{1,0:T(8,128)(2,1)S(1)} collective-permute-done((bf16[64,2048]{1,0:T(8,128)(2,1)S(1)}, bf16[64,2048]{1,0:T(8,128)(2,1)S(1)}, u32[]{:S(2)}, u32[]{:S(2)}) %collective-permute-start.6) | collective-permute-done | bytes 262176 | tf_op jit(solution)/shard_map/ppermute | solution.py:66
  21.1 0.1 collective-permute-start.7
  21.3 1.2 collective-permute-done.7.refs_0_
  22.5 6.4 %collective-permute-done.9.refs_0_ = bf16[64,2048]{1,0:T(8,128)(2,1)S(1)} collective-permute-done((bf16[64,2048]{1,0:T(8,128)(2,1)S(1)}, bf16[64,2048]{1,0:T(8,128)(2,1)S(1)}, u32[]{:S(2)}, u32[]{:S(2)}) %collective-permute-start.9) | collective-permute-done | bytes 262176 | tf_op jit(solution)/shard_map/ppermute | solution.py:66
  29.0 1.0 collective-permute-start.10
  30.0 1.7 %collective-permute-start.8 = (bf16[2,32,2048]{2,1,0:T(8,128)(2,1)S(1)}, bf16[2,32,2048]{2,1,0:T(8,128)(2,1)S(1)}, u32[]{:S(2)}, u32[]{:S(2)}) collective-permute-start(bf16[2,32,2048]{2,1,0:T(8,128)(2,1)S(1)} %pad_maximum_fusion), channel_id=1, source_target_pairs={{0,8},{1,9},{2,10},{3,11},{4,12},{5,13},{6,14},{7,15},{8,0},{9,1},... | collective-permute-start | bytes 786440 | tf_op jit(solution)/shard_map/ppermute | solution.py:44
  31.6 3.0 %collective-permute-done.17.value.refs_15_ = bf16[2,256,2048]{2,1,0:T(8,128)(2,1)S(1)} collective-permute-done((bf16[2,256,2048]{2,1,0:T(8,128)(2,1)S(1)}, bf16[2,256,2048]{2,1,0:T(8,128)(2,1)S(1)}, u32[]{:S(2)}, u32[]{:S(2)}) %collective-permute-start.17) | collective-permute-done | bytes 2097184 | tf_op jit(solution)/shard_map/ppermute | solution.py:66
  34.7 1.7 %collective-permute-start.19 = (bf16[256,2048]{1,0:T(8,128)(2,1)S(1)}, bf16[256,2048]{1,0:T(8,128)(2,1)S(1)}, u32[]{:S(2)}, u32[]{:S(2)}) collective-permute-start(bf16[256,2048]{1,0:T(8,128)(2,1)S(1)} %shard_map.83), channel_id=1, source_target_pairs={{0,32},{1,33},{2,34},{3,35},{4,36},{5,37},{6,38},{7,39},{8,40},{9,... | collective-permute-start | bytes 3145736 | tf_op jit(solution)/shard_map/ppermute | solution.py:66
  36.5 0.1 collective-permute-start.11
  36.6 0.1 collective-permute-start.13
  36.7 2.0 %collective-permute-done.8.refs_0_ = bf16[2,32,2048]{2,1,0:T(8,128)(2,1)S(1)} collective-permute-done((bf16[2,32,2048]{2,1,0:T(8,128)(2,1)S(1)}, bf16[2,32,2048]{2,1,0:T(8,128)(2,1)S(1)}, u32[]{:S(2)}, u32[]{:S(2)}) %collective-permute-start.8) | collective-permute-done | bytes 262176 | tf_op jit(solution)/shard_map/ppermute | solution.py:44
  38.7 2.9 %collective-permute-start.15 = (bf16[32,2048]{1,0:T(8,128)(2,1)S(1)}, bf16[32,2048]{1,0:T(8,128)(2,1)S(1)}, u32[]{:S(2)}, u32[]{:S(2)}) collective-permute-start(bf16[32,2048]{1,0:T(8,128)(2,1)S(1)} %bitcast.13), channel_id=1, source_target_pairs={{0,1},{1,2},{2,3},{3,4},{4,5},{5,6},{6,7},{7,0},{8,9},{9,10},{10,1... | collective-permute-start | bytes 393224 | tf_op jit(solution)/shard_map/ppermute | solution.py:66
  41.6 0.6 collective-permute-start.14
  42.2 3.7 %collective-permute-done.16 = bf16[32,2048]{1,0:T(8,128)(2,1)S(1)} collective-permute-done((bf16[32,2048]{1,0:T(8,128)(2,1)S(1)}, bf16[32,2048]{1,0:T(8,128)(2,1)S(1)}, u32[]{:S(2)}, u32[]{:S(2)}) %collective-permute-start.16) | collective-permute-done | bytes 131104 | tf_op jit(solution)/shard_map/ppermute | solution.py:66
  45.9 4.9 %collective-permute-done.19.refs_17_ = bf16[256,2048]{1,0:T(8,128)(2,1)S(1)} collective-permute-done((bf16[256,2048]{1,0:T(8,128)(2,1)S(1)}, bf16[256,2048]{1,0:T(8,128)(2,1)S(1)}, u32[]{:S(2)}, u32[]{:S(2)}) %collective-permute-start.19) | collective-permute-done | bytes 1048608 | tf_op jit(solution)/shard_map/ppermute | solution.py:66
  50.8 1.6 %copy-done.1 = bf16[1,1,1024,1024]{3,2,1,0:T(8,128)(2,1)S(1)} copy-done((bf16[1,1,1024,1024]{3,2,1,0:T(8,128)(2,1)S(1)}, bf16[1,1,1024,1024]{3,2,1,0:T(8,128)(2,1)}, u32[]{:S(2)}) %copy-start.1) | copy-done | bytes 2097176
  52.4 0.1 shard_map.86.own
  52.6 0.6 collective-permute-start.21
  53.2 0.3 collective-permute-done.20.refs_0_
  53.5 0.3 copy-done.3
  53.8 5.9 %shard_map.85.refs_0_ = bf16[8,128,1024]{2,1,0:T(8,128)(2,1)S(1)} custom-call(s32[16,16]{1,0:T(8,128)S(1)} %copy-done.5, bf16[1,32,2048]{2,1,0:T(8,128)(2,1)S(1)} %bitcast.17, bf16[1,32,2048]{2,1,0:T(8,128)(2,1)S(1)} %bitcast.16, bf16[1,32,2048]{2,1,0:T(8,128)(2,1)S(1)} %get-tuple-element.28.refs_2_, bf16[1,32,2048]{2,1,0:T(8,128)(2,1)S(1)} %shard_map.74.refs_1_.refs_3_, ...), custom_call_target="tpu_custom_call" | custom-call | flops 4294967296 | bytes 8388608 | tf_op jit(solution)/shard_map/pallas_call | solution.py:19
  59.7 33.9 %all_to_all.10.parts = bf16[8,128,1024]{2,1,0:T(8,128)(2,1)S(1)} all-to-all(bf16[8,128,1024]{2,1,0:T(8,128)(2,1)S(1)} %shard_map.87), channel_id=1, replica_groups={{0,32,64,96,128,160,192,224},{16,48,80,112,144,176,208,240},{1,33,65,97..., dimensions={0} | all-to-all | bytes 4194304 | tf_op jit(solution)/shard_map/all_to_all | solution.py:411
  93.6 0.2 shard_map.88.mine
  93.9 0.1 collective-permute-start.22
  94.0 0.9 shard_map.89
  94.9 1.7 %collective-permute-done.22.theirs = bf16[4,128,1024]{2,1,0:T(8,128)(2,1)S(1)} collective-permute-done((bf16[4,128,1024]{2,1,0:T(8,128)(2,1)S(1)}, bf16[4,128,1024]{2,1,0:T(8,128)(2,1)S(1)}, u32[]{:S(2)}, u32[]{:S(2)}) %collective-permute-start.22) | collective-permute-done | bytes 1048608 | tf_op jit(solution)/shard_map/ppermute | solution.py:39
  96.6 2.5 %shard_map.90 = (bf16[4,4,2,32,1024]{4,3,2,1,0:T(8,128)(2,1)S(1)}, bf16[8,64,1024]{2,1,0:T(8,128)(2,1)S(1)}) custom-call(bf16[4,128,1024]{2,1,0:T(8,128)(2,1)S(1)} %shard_map.88.mine, bf16[4,128,1024]{2,1,0:T(8,128)(2,1)S(1)} %collective-permute-done.22.theirs, bf16[512,1024]{1,0:T(8,128)(2,1)S(1)} %get-tuple-element.34.lrows, ...), custom_call_target="tpu_custom_call" | custom-call | flops 2147483648 | bytes 10485760 | tf_op jit(solution)/shard_map/pallas_call | solution.py:19
  99.1 20.2 %all_to_all.11.token.spread = bf16[8,64,1024]{2,1,0:T(8,128)(2,1)S(1)} all-to-all(bf16[8,64,1024]{2,1,0:T(8,128)(2,1)S(1)} %get-tuple-element.37), channel_id=1, replica_groups={{0,32,64,96,128,160,192,224},{16,48,80,112,144,176,208,240},{1,33,65,97..., dimensions={0} | all-to-all | bytes 2097152 | tf_op jit(solution)/shard_map/all_to_all | solution.py:414
  119.3 0.8 shard_map.92
  120.1 1.2 collective-permute-start.23
  121.3 0.9 collective-permute-start.24
  122.2 4.5 %collective-permute-start.25 = (bf16[2,64,1024]{2,1,0:T(8,128)(2,1)S(1)}, bf16[2,64,1024]{2,1,0:T(8,128)(2,1)S(1)}, u32[]{:S(2)}, u32[]{:S(2)}) collective-permute-start(bf16[2,64,1024]{2,1,0:T(8,128)(2,1)S(1)} %get-tuple-element.41), channel_id=1, source_target_pairs={{0,192},{16,208},{32,224},{48,240},{64,128},{80,144},{96,160},{112... | collective-permute-start | bytes 786440 | tf_op jit(solution)/shard_map/ppermute | solution.py:39
  126.7 5.0 %shard_map.91 = f32[1024,1024]{1,0:T(8,128)} custom-call(s32[16,16]{1,0:T(8,128)S(1)} %copy-done.5, bf16[1024,1024]{1,0:T(8,128)(2,1)S(1)} %bitcast.10, f32[1024,1024]{1,0:T(8,128)S(1)} %bitcast.9, bf16[8,64,1024]{2,1,0:T(8,128)(2,1)S(1)} %all_to_all.11.token.spread), custom_call_target="tpu_custom_call" | custom-call | flops 2147483648 | bytes 10485760 | tf_op jit(solution)/shard_map/pallas_call | solution.py:340
  131.7 3.2 %collective-permute-done.24.g2 = bf16[2,64,1024]{2,1,0:T(8,128)(2,1)S(1)} collective-permute-done((bf16[2,64,1024]{2,1,0:T(8,128)(2,1)S(1)}, bf16[2,64,1024]{2,1,0:T(8,128)(2,1)S(1)}, u32[]{:S(2)}, u32[]{:S(2)}) %collective-permute-start.24) | collective-permute-done | bytes 262176 | tf_op jit(solution)/shard_map/ppermute | solution.py:39
  134.9 1.1 shard_map.93
  (47 shorter events, 0.5 us)
Async XLA Ops:
  0.6 5.5 %collective-permute-start.5 = (bf16[256,2048]{1,0:T(8,128)(2,1)}, bf16[256,2048]{1,0:T(8,128)(2,1)S(1)}, u32[]{:S(2)}, u32[]{:S(2)}) collective-permute-start(bf16[256,2048]{1,0:T(8,128)(2,1)} %refs_13_.1), channel_id=1, source_target_pairs={{0,16},{16,0},{32,48},{48,32},{64,80},{80,64},{96,112},{112,96},{1... | collective-permute-start | bytes 3145736 | tf_op jit(solution)/shard_map/ppermute | solution.py:39
  0.7 0.9 copy-start.4
  1.7 4.4 %collective-permute-start = (bf16[64,256]{1,0:T(8,128)(2,1)S(1)}, bf16[64,256]{1,0:T(8,128)(2,1)S(1)}, u32[]{:S(2)}, u32[]{:S(2)}) collective-permute-start(bf16[64,256]{1,0:T(8,128)(2,1)S(1)} %get-tuple-element.23), channel_id=1, source_target_pairs={{0,32},{16,48},{32,64},{48,80},{64,96},{80,112},{96,0},{112,16},{1... | collective-permute-start | bytes 98312 | tf_op jit(solution)/shard_map/ppermute | solution.py:39
  3.3 6.9 %collective-permute-start.1 = (bf16[64,256]{1,0:T(8,128)(2,1)S(1)}, bf16[64,256]{1,0:T(8,128)(2,1)S(1)}, u32[]{:S(2)}, u32[]{:S(2)}) collective-permute-start(bf16[64,256]{1,0:T(8,128)(2,1)S(1)} %get-tuple-element.24), channel_id=1, source_target_pairs={{0,96},{16,112},{32,0},{48,16},{64,32},{80,48},{96,64},{112,80},{1... | collective-permute-start | bytes 98312 | tf_op jit(solution)/shard_map/ppermute | solution.py:39
  4.2 6.1 %collective-permute-start.2 = (bf16[64,256]{1,0:T(8,128)(2,1)S(1)}, bf16[64,256]{1,0:T(8,128)(2,1)S(1)}, u32[]{:S(2)}, u32[]{:S(2)}) collective-permute-start(bf16[64,256]{1,0:T(8,128)(2,1)S(1)} %get-tuple-element.25), channel_id=1, source_target_pairs={{0,64},{16,80},{32,96},{48,112},{64,0},{80,16},{96,32},{112,48},{1... | collective-permute-start | bytes 98312 | tf_op jit(solution)/shard_map/ppermute | solution.py:39
  6.2 1.2 copy-start.2
  7.5 27.1 %collective-permute-start.17 = (bf16[2,256,2048]{2,1,0:T(8,128)(2,1)S(1)}, bf16[2,256,2048]{2,1,0:T(8,128)(2,1)S(1)}, u32[]{:S(2)}, u32[]{:S(2)}) collective-permute-start(bf16[2,256,2048]{2,1,0:T(8,128)(2,1)S(1)} %shard_map.82), channel_id=1, source_target_pairs={{0,32},{1,33},{2,34},{3,35},{4,36},{5,37},{6,38},{7,39},{8,40},{9,... | collective-permute-start | bytes 6291464 | tf_op jit(solution)/shard_map/ppermute | solution.py:66
  10.3 1.4 %collective-permute-start.3 = (bf16[64,1024]{1,0:T(8,128)(2,1)S(1)}, bf16[64,1024]{1,0:T(8,128)(2,1)S(1)}, u32[]{:S(2)}, u32[]{:S(2)}) collective-permute-start(bf16[64,1024]{1,0:T(8,128)(2,1)S(1)} %shard_map.69.half), channel_id=1, source_target_pairs={{0,16},{16,0},{32,48},{48,32},{64,80},{80,64},{96,112},{112,96},{1... | collective-permute-start | bytes 393224 | tf_op jit(solution)/shard_map/ppermute | solution.py:39
  11.7 9.3 %collective-permute-start.6 = (bf16[64,2048]{1,0:T(8,128)(2,1)S(1)}, bf16[64,2048]{1,0:T(8,128)(2,1)S(1)}, u32[]{:S(2)}, u32[]{:S(2)}) collective-permute-start(bf16[64,2048]{1,0:T(8,128)(2,1)S(1)} %shard_map.72), channel_id=1, source_target_pairs={{0,1},{1,2},{2,3},{3,4},{4,5},{5,6},{6,7},{7,0},{8,9},{9,10},{10,1... | collective-permute-start | bytes 786440 | tf_op jit(solution)/shard_map/ppermute | solution.py:66
  12.8 8.4 %collective-permute-start.4 = (bf16[32,2048]{1,0:T(8,128)(2,1)S(1)}, bf16[32,2048]{1,0:T(8,128)(2,1)S(1)}, u32[]{:S(2)}, u32[]{:S(2)}) collective-permute-start(bf16[32,2048]{1,0:T(8,128)(2,1)S(1)} %get-tuple-element.26), channel_id=1, source_target_pairs={{0,8},{1,9},{2,10},{3,11},{4,12},{5,13},{6,14},{7,15},{8,0},{9,1},... | collective-permute-start | bytes 393224 | tf_op jit(solution)/shard_map/ppermute | solution.py:44
  21.1 1.4 %collective-permute-start.7 = (bf16[1,32,2048]{2,1,0:T(8,128)(2,1)S(1)}, bf16[1,32,2048]{2,1,0:T(8,128)(2,1)S(1)}, u32[]{:S(2)}, u32[]{:S(2)}) collective-permute-start(bf16[1,32,2048]{2,1,0:T(8,128)(2,1)S(1)} %get-tuple-element.29), channel_id=1, source_target_pairs={{0,16},{16,0},{32,48},{48,32},{64,80},{80,64},{96,112},{112,96},{1... | collective-permute-start | bytes 393224 | tf_op jit(solution)/shard_map/ppermute | solution.py:39
  21.2 7.7 %collective-permute-start.9 = (bf16[64,2048]{1,0:T(8,128)(2,1)S(1)}, bf16[64,2048]{1,0:T(8,128)(2,1)S(1)}, u32[]{:S(2)}, u32[]{:S(2)}) collective-permute-start(bf16[64,2048]{1,0:T(8,128)(2,1)S(1)} %shard_map.76), channel_id=1, source_target_pairs={{0,1},{1,2},{2,3},{3,4},{4,5},{5,6},{6,7},{7,0},{8,9},{9,10},{10,1... | collective-permute-start | bytes 786440 | tf_op jit(solution)/shard_map/ppermute | solution.py:66
  28.9 7.7 %collective-permute-start.12 = (bf16[64,2048]{1,0:T(8,128)(2,1)S(1)}, bf16[64,2048]{1,0:T(8,128)(2,1)S(1)}, u32[]{:S(2)}, u32[]{:S(2)}) collective-permute-start(bf16[64,2048]{1,0:T(8,128)(2,1)S(1)} %shard_map.78), channel_id=1, source_target_pairs={{0,1},{1,2},{2,3},{3,4},{4,5},{5,6},{6,7},{7,0},{8,9},{9,10},{10,1... | collective-permute-start | bytes 786440 | tf_op jit(solution)/shard_map/ppermute | solution.py:66
  29.0 7.4 %collective-permute-start.10 = (bf16[1,32,2048]{2,1,0:T(8,128)(2,1)S(1)}, bf16[1,32,2048]{2,1,0:T(8,128)(2,1)S(1)}, u32[]{:S(2)}, u32[]{:S(2)}) collective-permute-start(bf16[1,32,2048]{2,1,0:T(8,128)(2,1)S(1)} %get-tuple-element.31), channel_id=1, source_target_pairs={{0,16},{16,0},{32,48},{48,32},{64,80},{80,64},{96,112},{112,96},{1... | collective-permute-start | bytes 393224 | tf_op jit(solution)/shard_map/ppermute | solution.py:39
  30.0 8.8 %collective-permute-start.8 = (bf16[2,32,2048]{2,1,0:T(8,128)(2,1)S(1)}, bf16[2,32,2048]{2,1,0:T(8,128)(2,1)S(1)}, u32[]{:S(2)}, u32[]{:S(2)}) collective-permute-start(bf16[2,32,2048]{2,1,0:T(8,128)(2,1)S(1)} %pad_maximum_fusion), channel_id=1, source_target_pairs={{0,8},{1,9},{2,10},{3,11},{4,12},{5,13},{6,14},{7,15},{8,0},{9,1},... | collective-permute-start | bytes 786440 | tf_op jit(solution)/shard_map/ppermute | solution.py:44
  34.7 16.1 %collective-permute-start.19 = (bf16[256,2048]{1,0:T(8,128)(2,1)S(1)}, bf16[256,2048]{1,0:T(8,128)(2,1)S(1)}, u32[]{:S(2)}, u32[]{:S(2)}) collective-permute-start(bf16[256,2048]{1,0:T(8,128)(2,1)S(1)} %shard_map.83), channel_id=1, source_target_pairs={{0,32},{1,33},{2,34},{3,35},{4,36},{5,37},{6,38},{7,39},{8,40},{9,... | collective-permute-start | bytes 3145736 | tf_op jit(solution)/shard_map/ppermute | solution.py:66
  36.5 17.0 %collective-permute-start.11 = (bf16[2,32,2048]{2,1,0:T(8,128)(2,1)S(1)}, bf16[2,32,2048]{2,1,0:T(8,128)(2,1)S(1)}, u32[]{:S(2)}, u32[]{:S(2)}) collective-permute-start(bf16[2,32,2048]{2,1,0:T(8,128)(2,1)S(1)} %pad_maximum_fusion.1), channel_id=1, source_target_pairs={{0,8},{1,9},{2,10},{3,11},{4,12},{5,13},{6,14},{7,15},{8,0},{9,1},... | collective-permute-start | bytes 786440 | tf_op jit(solution)/shard_map/ppermute | solution.py:44
  36.6 5.0 %collective-permute-start.13 = (bf16[1,32,2048]{2,1,0:T(8,128)(2,1)S(1)}, bf16[1,32,2048]{2,1,0:T(8,128)(2,1)S(1)}, u32[]{:S(2)}, u32[]{:S(2)}) collective-permute-start(bf16[1,32,2048]{2,1,0:T(8,128)(2,1)S(1)} %get-tuple-element.33), channel_id=1, source_target_pairs={{0,16},{16,0},{32,48},{48,32},{64,80},{80,64},{96,112},{112,96},{1... | collective-permute-start | bytes 393224 | tf_op jit(solution)/shard_map/ppermute | solution.py:39
  38.7 7.2 %collective-permute-start.16 = (bf16[32,2048]{1,0:T(8,128)(2,1)S(1)}, bf16[32,2048]{1,0:T(8,128)(2,1)S(1)}, u32[]{:S(2)}, u32[]{:S(2)}) collective-permute-start(bf16[32,2048]{1,0:T(8,128)(2,1)S(1)} %bitcast.12), channel_id=1, source_target_pairs={{0,9},{1,10},{2,11},{3,12},{4,13},{5,14},{6,15},{7,8},{8,1},{9,2},... | collective-permute-start | bytes 393224 | tf_op jit(solution)/shard_map/ppermute | solution.py:66
  38.7 12.1 %collective-permute-start.15 = (bf16[32,2048]{1,0:T(8,128)(2,1)S(1)}, bf16[32,2048]{1,0:T(8,128)(2,1)S(1)}, u32[]{:S(2)}, u32[]{:S(2)}) collective-permute-start(bf16[32,2048]{1,0:T(8,128)(2,1)S(1)} %bitcast.13), channel_id=1, source_target_pairs={{0,1},{1,2},{2,3},{3,4},{4,5},{5,6},{6,7},{7,0},{8,9},{9,10},{10,1... | collective-permute-start | bytes 393224 | tf_op jit(solution)/shard_map/ppermute | solution.py:66
  41.6 11.9 %collective-permute-start.14 = (bf16[2,32,2048]{2,1,0:T(8,128)(2,1)S(1)}, bf16[2,32,2048]{2,1,0:T(8,128)(2,1)S(1)}, u32[]{:S(2)}, u32[]{:S(2)}) collective-permute-start(bf16[2,32,2048]{2,1,0:T(8,128)(2,1)S(1)} %pad_maximum_fusion.2), channel_id=1, source_target_pairs={{0,8},{1,9},{2,10},{3,11},{4,12},{5,13},{6,14},{7,15},{8,0},{9,1},... | collective-permute-start | bytes 786440 | tf_op jit(solution)/shard_map/ppermute | solution.py:44
  45.9 7.6 %collective-permute-start.18 = (bf16[2,256,2048]{2,1,0:T(8,128)(2,1)S(1)}, bf16[2,256,2048]{2,1,0:T(8,128)(2,1)S(1)}, u32[]{:S(2)}, u32[]{:S(2)}) collective-permute-start(bf16[2,256,2048]{2,1,0:T(8,128)(2,1)S(1)} %collective-permute-done.17.value.refs_15_), channel_id=1, source_target_pairs={{0,16},{16,0},{32,48},{48,32},{64,80},{80,64},{96,112},{112,96},{1... | collective-permute-start | bytes 6291464 | tf_op jit(solution)/shard_map/ppermute | solution.py:39
  50.8 2.7 %collective-permute-start.20 = (bf16[256,2048]{1,0:T(8,128)(2,1)S(1)}, bf16[256,2048]{1,0:T(8,128)(2,1)S(1)}, u32[]{:S(2)}, u32[]{:S(2)}) collective-permute-start(bf16[256,2048]{1,0:T(8,128)(2,1)S(1)} %collective-permute-done.19.refs_17_), channel_id=1, source_target_pairs={{0,16},{16,0},{32,48},{48,32},{64,80},{80,64},{96,112},{112,96},{1... | collective-permute-start | bytes 3145736 | tf_op jit(solution)/shard_map/ppermute | solution.py:39
  50.8 1.6 %copy-start.1 = (bf16[1,1,1024,1024]{3,2,1,0:T(8,128)(2,1)S(1)}, bf16[1,1,1024,1024]{3,2,1,0:T(8,128)(2,1)}, u32[]{:S(2)}) copy-start(bf16[1,1,1024,1024]{3,2,1,0:T(8,128)(2,1)} %param.9) | copy-start | bytes 6291460
  52.6 1.2 copy-start.3
  52.6 1.2 copy-start.5
  52.6 7.1 %collective-permute-start.21 = (bf16[1024,1024]{1,0:T(8,128)(2,1)S(1)}, bf16[1024,1024]{1,0:T(8,128)(2,1)S(1)}, u32[]{:S(2)}, u32[]{:S(2)}) collective-permute-start(bf16[1024,1024]{1,0:T(8,128)(2,1)S(1)} %shard_map.86.own), channel_id=1, source_target_pairs={{0,16},{16,0},{32,48},{48,32},{64,80},{80,64},{96,112},{112,96},{1... | collective-permute-start | bytes 6291464 | tf_op jit(solution)/shard_map/ppermute | solution.py:39
  93.9 2.7 %collective-permute-start.22 = (bf16[4,128,1024]{2,1,0:T(8,128)(2,1)S(1)}, bf16[4,128,1024]{2,1,0:T(8,128)(2,1)S(1)}, u32[]{:S(2)}, u32[]{:S(2)}) collective-permute-start(bf16[4,128,1024]{2,1,0:T(8,128)(2,1)S(1)} %shard_map.88.mine), channel_id=1, source_target_pairs={{0,16},{16,0},{32,48},{48,32},{64,80},{80,64},{96,112},{112,96},{1... | collective-permute-start | bytes 3145736 | tf_op jit(solution)/shard_map/ppermute | solution.py:39
  96.6 30.1 %copy-start = (f32[1,1,1024,1024]{3,2,1,0:T(8,128)S(1)}, f32[1,1,1024,1024]{3,2,1,0:T(8,128)}, u32[]{:S(2)}) copy-start(f32[1,1,1024,1024]{3,2,1,0:T(8,128)} %param.8) | copy-start | bytes 12582916
  120.1 11.6 %collective-permute-start.23 = (bf16[2,64,1024]{2,1,0:T(8,128)(2,1)S(1)}, bf16[2,64,1024]{2,1,0:T(8,128)(2,1)S(1)}, u32[]{:S(2)}, u32[]{:S(2)}) collective-permute-start(bf16[2,64,1024]{2,1,0:T(8,128)(2,1)S(1)} %get-tuple-element.39), channel_id=1, source_target_pairs={{0,64},{16,80},{32,96},{48,112},{64,0},{80,16},{96,32},{112,48},{1... | collective-permute-start | bytes 786440 | tf_op jit(solution)/shard_map/ppermute | solution.py:39
  121.3 13.6 %collective-permute-start.24 = (bf16[2,64,1024]{2,1,0:T(8,128)(2,1)S(1)}, bf16[2,64,1024]{2,1,0:T(8,128)(2,1)S(1)}, u32[]{:S(2)}, u32[]{:S(2)}) collective-permute-start(bf16[2,64,1024]{2,1,0:T(8,128)(2,1)S(1)} %get-tuple-element.40), channel_id=1, source_target_pairs={{0,128},{16,144},{32,160},{48,176},{64,192},{80,208},{96,224},{112... | collective-permute-start | bytes 786440 | tf_op jit(solution)/shard_map/ppermute | solution.py:39
  122.2 12.7 %collective-permute-start.25 = (bf16[2,64,1024]{2,1,0:T(8,128)(2,1)S(1)}, bf16[2,64,1024]{2,1,0:T(8,128)(2,1)S(1)}, u32[]{:S(2)}, u32[]{:S(2)}) collective-permute-start(bf16[2,64,1024]{2,1,0:T(8,128)(2,1)S(1)} %get-tuple-element.41), channel_id=1, source_target_pairs={{0,192},{16,208},{32,224},{48,240},{64,128},{80,144},{96,160},{112... | collective-permute-start | bytes 786440 | tf_op jit(solution)/shard_map/ppermute | solution.py:39
